TPU v7x, 128 devices: a whole 4x4x4 slice. The times are simulated.
128 devices in a mesh: nz: 4 (over y_hi, core), nx: 32 (over z, y_lo, x).
Axes of the slice: x: 4, y: 4 (y_hi: 2, y_lo: 2; y = y_hi * 2 + y_lo), z: 4, core: 2. Of those that a mesh axis runs over, the one named last changes fastest.
Arguments:
- phi_hat: bfloat16 [344, 704, 513], P('nz', 'nx'), may hold values from -6 to 6
- vel_hat: bfloat16 [344, 704, 513], P('nz', 'nx'), may hold values from -6 to 6
- helm_basis: bfloat16 [513, 513], replicated, may hold values from -0.25 to 0.25
- helm_dual: bfloat16 [513, 513], replicated, may hold values from -0.25 to 0.25
- helm_rates: float32 [513], replicated, may hold values from 0.5 to 20
Outputs:
- phi_new: float32 [344, 704, 513], P('nz', 'nx')
All inputs are finite; a program needn't handle non-finite values.
Results may differ from a plain program's by a relative error of at most 0.035.
Values may be sent and summed in bfloat16 or wider, within the bound.
A program may use at most 128 MiB of HBM per device.

v0:
```python
import math

import jax
import jax.numpy as jnp
from jax import lax
from jax.sharding import PartitionSpec as P

NX = 1024
NZ = 512


mobility = 1.0
capillary = 0.2
screen_low = 4.0
screen_high = 20.0
time_step = 1.0 / (screen_low * screen_high * mobility * capillary)
stabilizer = capillary * (screen_low + screen_high)


def fourier_tables(mode_count, point_count):
    half_count = mode_count // 2
    mode_index = jnp.arange(mode_count, dtype=jnp.int32)
    point_index = jnp.arange(point_count, dtype=jnp.int32)
    wave_index = jnp.where(mode_index < half_count, mode_index, mode_index - half_count + 1)
    phase_steps = wave_index[:, None] * point_index[None, :] % point_count
    angles = phase_steps.astype(jnp.float32) * (2.0 * math.pi / point_count)
    basis = jnp.where((mode_index < half_count)[:, None], jnp.cos(angles), jnp.sin(angles))
    factor = math.sqrt(2.0 / mode_count)
    synthesis = (factor * basis).astype(jnp.bfloat16)
    weights = jnp.where(mode_index == 0, 1.0, 2.0).astype(jnp.float32) / (point_count * factor)
    analysis = (basis.T * weights[None, :]).astype(jnp.bfloat16)
    wavenumber = 2.0 * wave_index.astype(jnp.float32) / half_count
    return (synthesis, analysis, wavenumber)


def chebyshev_tables(count):
    index = jnp.arange(count, dtype=jnp.int32)
    period = 2 * (count - 1)
    phase_steps = index[:, None] * index[None, :] % period
    cosines = jnp.cos(phase_steps.astype(jnp.float32) * (math.pi / (count - 1)))
    factor = math.sqrt(2.0 / count)
    synthesis = (factor * cosines).astype(jnp.bfloat16)
    ends = jnp.where((index == 0) | (index == count - 1), 2.0, 1.0).astype(jnp.float32)
    analysis = (
        cosines.T * (2.0 / ((count - 1) * factor)) / (ends[:, None] * ends[None, :])
    ).astype(jnp.bfloat16)
    upper = index[:, None]
    lower = index[None, :]
    deriv = jnp.where(
        (upper > lower) & ((upper + lower) % 2 == 1),
        2.0 * upper.astype(jnp.float32) / ends[None, :],
        0.0,
    )
    return (synthesis, analysis, deriv.astype(jnp.bfloat16))


def along(values, table, which):
    forms = ("kab,kz->zab", "akb,kz->azb", "abk,kz->abz")
    return jnp.einsum(forms[which], values, table, preferred_element_type=jnp.float32)


def products(phi_phys, vel_phys):
    cube = (phi_phys * phi_phys * phi_phys).astype(jnp.bfloat16)
    flux = (vel_phys * phi_phys).astype(jnp.bfloat16)
    return (cube, flux)


def per_device(phi_hat, vel_hat, helm_basis, helm_dual, helm_rates):
    span_count = lax.axis_size("nz")
    stream_count = lax.axis_size("nx")
    span_local, stream_local, cheb_count = phi_hat.shape
    span_modes = span_local * span_count
    stream_modes = stream_local * stream_count
    synth_x, analy_x, wave_x = fourier_tables(stream_modes, NX)
    synth_z, analy_z, wave_z = fourier_tables(span_modes, NZ)
    synth_y, analy_y, deriv_y = chebyshev_tables(cheb_count)
    phi_points = along(phi_hat, synth_y, 2).astype(jnp.bfloat16)
    vel_points = along(vel_hat, synth_y, 2).astype(jnp.bfloat16)
    extra = -cheb_count % span_count
    phi_padded = jnp.pad(phi_points, ((0, 0), (0, 0), (0, extra)))
    vel_padded = jnp.pad(vel_points, ((0, 0), (0, 0), (0, extra)))
    pieces = (
        lax.all_to_all(phi_padded, "nz", split_axis=2, concat_axis=0, tiled=True),
        lax.all_to_all(vel_padded, "nz", split_axis=2, concat_axis=0, tiled=True),
    )
    phi_span = along(pieces[0], synth_z, 0).astype(jnp.bfloat16)
    vel_span = along(pieces[1], synth_z, 0).astype(jnp.bfloat16)
    pieces = (
        lax.all_to_all(phi_span, "nx", split_axis=0, concat_axis=1, tiled=True),
        lax.all_to_all(vel_span, "nx", split_axis=0, concat_axis=1, tiled=True),
    )
    cube, flux = products(along(pieces[0], synth_x, 1), along(pieces[1], synth_x, 1))
    cube_stream = along(cube, analy_x, 1).astype(jnp.bfloat16)
    flux_stream = along(flux, analy_x, 1).astype(jnp.bfloat16)
    pieces = (
        lax.all_to_all(cube_stream, "nx", split_axis=1, concat_axis=0, tiled=True),
        lax.all_to_all(flux_stream, "nx", split_axis=1, concat_axis=0, tiled=True),
    )
    cube_span = along(pieces[0], analy_z, 0).astype(jnp.bfloat16)
    flux_span = along(pieces[1], analy_z, 0).astype(jnp.bfloat16)
    pieces = (
        lax.all_to_all(cube_span, "nz", split_axis=0, concat_axis=2, tiled=True),
        lax.all_to_all(flux_span, "nz", split_axis=0, concat_axis=2, tiled=True),
    )
    cube_hat = along(pieces[0][:, :, :cheb_count], analy_y, 2)
    flux_hat = along(pieces[1][:, :, :cheb_count], analy_y, 2)
    wave_stream = lax.dynamic_slice_in_dim(
        wave_x, lax.axis_index("nx") * stream_local, stream_local
    )
    wave_span = lax.dynamic_slice_in_dim(wave_z, lax.axis_index("nz") * span_local, span_local)
    squares = (
        wave_span[:, None] * wave_span[:, None] + wave_stream[None, :] * wave_stream[None, :]
    )[:, :, None]
    eigen = -helm_rates[None, None, :]
    dual_table = helm_dual.T
    basis_table = helm_basis.T
    phi_float = phi_hat.astype(jnp.float32)
    source = (cube_hat - (1.0 + stabilizer) * phi_float).astype(jnp.bfloat16)
    slope = along(flux_hat.astype(jnp.bfloat16), deriv_y, 2)
    scaled = ((eigen - squares) * along(source, dual_table, 2)).astype(jnp.bfloat16)
    lap_part = along(scaled, basis_table, 2)
    forcing = (
        (phi_float / time_step + mobility * lap_part - 8.0 / (cheb_count - 1) * slope)
        / (capillary * mobility)
    ).astype(jnp.bfloat16)
    first = (along(forcing, dual_table, 2) / (eigen - squares - screen_low)).astype(jnp.bfloat16)
    middle = along(first, basis_table, 2).astype(jnp.bfloat16)
    second = (along(middle, dual_table, 2) / (eigen - squares - screen_high)).astype(jnp.bfloat16)
    return along(second, basis_table, 2)


def solution(mesh):
    placed = (P("nz", "nx", None), P("nz", "nx", None), P(), P(), P())
    return jax.shard_map(
        per_device, mesh=mesh, in_specs=placed, out_specs=P("nz", "nx", None), check_vma=False
    )
```

profile of v0, /device:TPU:1, one launch (start us, length us, event | category | flops | bytes accessed | tf_op | source)
XLA Modules:
  0.0 587.2 jit_solution(4644020064925415614)
XLA Ops:
  0.0 11.1 %convert_bitcast_fusion.3 = bf16[86,22,513]{2,0,1:T(8,128)(2,1)} fusion(bf16[86,22,513]{2,0,1:T(8,128)(2,1)} %param.5), kind=kOutput, calls=%fused_computation.63 | convolution fusion | flops 1001012800 | bytes 3882384 | tf_op jit(solution)/shard_map/abk,kz->abz/dot_general | solution.py:59
  11.1 5.6 copy.64
  16.7 4.2 pad.7.clone
  20.9 6.0 %all-to-all-start = ((bf16[86,22,516]{0,1,2:T(8,128)(2,1)}), bf16[86,22,516]{0,1,2:T(8,128)(2,1)}, u32[]{:S(2)}, u32[]{:S(2)}) async-start(bf16[86,22,516]{0,1,2:T(8,128)(2,1)} %pad.7.clone), calls=%async_computation | async-start | bytes 6340608 | tf_op jit(solution)/shard_map/all_to_all | solution.py:83
  26.9 9.3 %convert_bitcast_fusion.2 = bf16[86,22,513]{2,0,1:T(8,128)(2,1)} fusion(bf16[86,22,513]{2,0,1:T(8,128)(2,1)S(1)} %copy-done), kind=kOutput, calls=%fused_computation.61 | convolution fusion | flops 1001012800 | bytes 3882384 | tf_op jit(solution)/shard_map/abk,kz->abz/dot_general | solution.py:59
  36.3 5.6 copy.65
  41.9 4.2 pad.8.clone
  46.1 18.8 %all-to-all-done = bf16[86,22,516]{0,1,2:T(8,128)(2,1)} async-done(((bf16[86,22,516]{0,1,2:T(8,128)(2,1)}), bf16[86,22,516]{0,1,2:T(8,128)(2,1)}, u32[]{:S(2)}, u32[]{:S(2)}) %all-to-all-start) | async-done | bytes 1952576 | tf_op jit(solution)/shard_map/all_to_all | solution.py:83
  64.9 5.7 all-to-all-start.4
  70.6 4.6 copy.30
  75.2 5.2 all_to_all.107
  80.4 6.0 %convolution_convert_fusion.1 = bf16[512,22,129]{0,2,1:T(8,128)(2,1)} fusion(bf16[344,22,129]{0,2,1:T(8,128)(2,1)S(1)} %all_to_all.107, s32[344]{0:T(512)S(1)} %iota_select_fusion.1, pred[344]{0:T(512)(128)(4,1)S(1)} %iota_compare_fusion.5), kind=kOutput, calls=%fused_computation.70 | convolution fusion | flops 1004149760 | bytes 4860376 | tf_op jit(solution)/shard_map/kab,kz->zab/dot_general | solution.py:59
  86.3 9.1 %copy.31 = bf16[512,22,129]{2,1,0:T(8,128)(2,1)} copy(bf16[512,22,129]{0,2,1:T(8,128)(2,1)} %convolution_convert_fusion.1) | data formatting | bytes 5812224 | tf_op jit(solution)/shard_map/convert_element_type | solution.py:86
  95.4 11.6 %reshape.97 = bf16[32,2,22704]{2,1,0:T(2,128)(2,1)} reshape(bf16[512,22,129]{2,1,0:T(8,128)(2,1)} %copy.31) | data formatting | bytes 5812224
  107.0 1.5 all-to-all-done.4
  108.5 9.3 %all-to-all-start.1 = ((bf16[32,2,22704]{2,1,0:T(2,128)(2,1)}), bf16[32,2,22704]{2,1,0:T(2,128)(2,1)}, u32[]{:S(2)}, u32[]{:S(2)}) async-start(bf16[32,2,22704]{2,1,0:T(2,128)(2,1)} %reshape.97), calls=%async_computation.1 | async-start | bytes 5832704 | tf_op jit(solution)/shard_map/all_to_all | solution.py:89
  117.8 4.6 copy.43
  122.4 5.2 all_to_all.123
  127.6 6.0 %convolution_convert_fusion = bf16[512,22,129]{0,2,1:T(8,128)(2,1)} fusion(bf16[344,22,129]{0,2,1:T(8,128)(2,1)S(1)} %all_to_all.123, s32[344]{0:T(512)S(1)} %iota_select_fusion.1, pred[344]{0:T(512)(128)(4,1)S(1)} %iota_compare_fusion.5), kind=kOutput, calls=%fused_computation.69 | convolution fusion | flops 1004149760 | bytes 4860376 | tf_op jit(solution)/shard_map/kab,kz->zab/dot_general | solution.py:59
  133.5 9.1 %copy.44 = bf16[512,22,129]{2,1,0:T(8,128)(2,1)} copy(bf16[512,22,129]{0,2,1:T(8,128)(2,1)} %convolution_convert_fusion) | data formatting | bytes 5812224 | tf_op jit(solution)/shard_map/convert_element_type | solution.py:87
  142.6 11.6 %reshape.99 = bf16[32,2,22704]{2,1,0:T(2,128)(2,1)} reshape(bf16[512,22,129]{2,1,0:T(8,128)(2,1)} %copy.44) | data formatting | bytes 5812224
  154.2 0.0 all-to-all-done.1
  154.2 8.8 %all-to-all-start.5 = ((bf16[32,2,22704]{2,1,0:T(2,128)(2,1)}), bf16[32,2,22704]{2,1,0:T(2,128)(2,1)}, u32[]{:S(2)}, u32[]{:S(2)}) async-start(bf16[32,2,22704]{2,1,0:T(2,128)(2,1)} %reshape.99), calls=%async_computation.5 | async-start | bytes 5832704 | tf_op jit(solution)/shard_map/all_to_all | solution.py:90
  163.1 12.7 %fusion.269 = bf16[1024,704,1]{0,1,2:T(8,128)(2,1)S(1)} fusion(f32[704]{0:T(1024)S(1)} %select_multiply_fusion, s32[704]{0:T(1024)S(1)} %iota_select_fusion, pred[704]{0:T(1024)(128)(4,1)S(1)} %iota_compare_fusion.1), kind=kLoop, calls=%fused_computation.82.clone.clone.2 | loop fusion | flops 12255232 | bytes 1448128 | tf_op jit(solution)/shard_map/akb,kz->azb/dot_general | solution.py:59
  175.8 14.4 %reshape.98 = bf16[512,22,129]{2,1,0:T(8,128)(2,1)} reshape(bf16[32,2,22704]{2,1,0:T(2,128)(2,1)} %all-to-all-done.1) | data formatting | bytes 5812224
  190.2 4.6 copy.33
  194.8 20.2 %fusion.4 = f32[1024,16,129]{0,2,1:T(8,128)} fusion(bf16[16,704,129]{2,0,1:T(8,128)(2,1)S(1)} %bitcast.147, s32[704]{0:T(1024)S(1)} %iota_select_fusion, pred[704]{0:T(1024)(128)(4,1)S(1)} %iota_compare_fusion.1), kind=kOutput, calls=%fused_computation.11 | convolution fusion | flops 2988113920 | bytes 11363776 | tf_op jit(solution)/shard_map/akb,kz->azb/dot_general | solution.py:59
  215.0 14.3 %reshape.100 = bf16[512,22,129]{2,1,0:T(8,128)(2,1)} reshape(bf16[32,2,22704]{2,1,0:T(2,128)(2,1)} %all-to-all-done.5) | data formatting | bytes 5812224
  229.4 7.0 %copy.46 = bf16[16,32,22,129]{3,0,2,1:T(8,128)(2,1)} copy(bf16[16,32,22,129]{3,2,0,1:T(8,128)(2,1)} %bitcast.140) | data formatting | bytes 5812224 | tf_op jit(solution)/shard_map/all_to_all | solution.py:90
  236.4 27.8 %convert_bitcast_fusion = bf16[16,704,129]{1,2,0:T(8,128)(2,1)} fusion(f32[1024,16,129]{0,2,1:T(8,128)} %fusion.4, bf16[16,704,129]{2,0,1:T(8,128)(2,1)} %bitcast.146, s32[704]{0:T(1024)S(1)} %iota_select_fusion, pred[704]{0:T(1024)(128)(4,1)S(1)} %iota_compare_fusion.1, bf16[1024,704,1]{0,1,2:T(8,128)(2,1)S(1)} %fusion.269), kind=kOutput, calls=%fused_computation.32 | convolution fusion | flops 5969652736 | bytes 15711680 | tf_op jit(solution)/shard_map/akb,kz->azb/dot_general | solution.py:59
  264.2 8.9 %copy.48 = bf16[16,704,129]{2,0,1:T(8,128)(2,1)} copy(bf16[16,704,129]{1,2,0:T(8,128)(2,1)} %convert_bitcast_fusion) | data formatting | bytes 5812224 | tf_op jit(solution)/shard_map/convert_element_type | solution.py:94
  273.1 8.2 %all-to-all-start.6 = ((bf16[16,704,129]{2,0,1:T(8,128)(2,1)}), bf16[16,704,129]{2,0,1:T(8,128)(2,1)}, u32[]{:S(2)}, u32[]{:S(2)}) async-start(bf16[16,704,129]{2,0,1:T(8,128)(2,1)} %copy.48), calls=%async_computation.6 | async-start | bytes 11534336 | tf_op jit(solution)/shard_map/all_to_all | solution.py:97
  281.3 4.9 fusion.271
  286.2 16.0 %convert_bitcast_fusion.1 = bf16[16,704,129]{1,2,0:T(8,128)(2,1)} fusion(f32[704]{0:T(1024)S(1)} %select_multiply_fusion, s32[704]{0:T(1024)S(1)} %iota_select_fusion, pred[704]{0:T(1024)(128)(4,1)S(1)} %iota_compare_fusion.1, bf16[16,1024,129]{1,2,0:T(8,128)(2,1)S(1)} %fusion.271), kind=kOutput, calls=%fused_computation.33 | convolution fusion | flops 2989566976 | bytes 7139520 | tf_op jit(solution)/shard_map/akb,kz->azb/dot_general | solution.py:59
  302.1 8.9 %copy.35 = bf16[16,704,129]{2,0,1:T(8,128)(2,1)} copy(bf16[16,704,129]{1,2,0:T(8,128)(2,1)} %convert_bitcast_fusion.1) | data formatting | bytes 5812224 | tf_op jit(solution)/shard_map/convert_element_type | solution.py:93
  311.1 46.3 %all-to-all-done.6 = bf16[16,704,129]{2,0,1:T(8,128)(2,1)} async-done(((bf16[16,704,129]{2,0,1:T(8,128)(2,1)}), bf16[16,704,129]{2,0,1:T(8,128)(2,1)}, u32[]{:S(2)}, u32[]{:S(2)}) %all-to-all-start.6) | async-done | bytes 2906144 | tf_op jit(solution)/shard_map/all_to_all | solution.py:97
  357.4 7.2 %all-to-all-start.2 = ((bf16[16,704,129]{2,0,1:T(8,128)(2,1)}), bf16[16,704,129]{2,0,1:T(8,128)(2,1)}, u32[]{:S(2)}, u32[]{:S(2)}) async-start(bf16[16,704,129]{2,0,1:T(8,128)(2,1)} %copy.35), calls=%async_computation.2 | async-start | bytes 11534336 | tf_op jit(solution)/shard_map/all_to_all | solution.py:96
  364.5 3.2 copy.49
  367.8 5.1 convolution_convert_fusion.2
  372.9 4.8 copy.51
  377.7 9.4 %reshape.101 = bf16[4,2,122034]{2,1,0:T(2,128)(2,1)} reshape(bf16[344,22,129]{2,1,0:T(8,128)(2,1)} %copy.51) | data formatting | bytes 3905088
  387.0 54.2 %all-to-all-done.2 = bf16[16,704,129]{2,0,1:T(8,128)(2,1)} async-done(((bf16[16,704,129]{2,0,1:T(8,128)(2,1)}), bf16[16,704,129]{2,0,1:T(8,128)(2,1)}, u32[]{:S(2)}, u32[]{:S(2)}) %all-to-all-start.2) | async-done | bytes 2906144 | tf_op jit(solution)/shard_map/all_to_all | solution.py:96
  441.2 9.0 %all-to-all-start.7 = ((bf16[4,2,122034]{2,1,0:T(2,128)(2,1)}), bf16[4,2,122034]{2,1,0:T(2,128)(2,1)S(1)}, u32[]{:S(2)}, u32[]{:S(2)}) async-start(bf16[4,2,122034]{2,1,0:T(2,128)(2,1)} %reshape.101), calls=%async_computation.7 | async-start | bytes 3907584 | tf_op jit(solution)/shard_map/all_to_all | solution.py:103
  450.2 3.2 copy.36
  453.5 10.1 %convolution_convert_fusion.3 = bf16[344,22,129]{0,2,1:T(8,128)(2,1)} fusion(bf16[512,22,129]{2,0,1:T(8,128)(2,1)S(1)} %bitcast.145, f32[344]{0:T(512)S(1)} %select_multiply_fusion.1, s32[344]{0:T(512)S(1)} %iota_select_fusion.1, pred[344]{0:T(512)(128)(4,1)S(1)} %iota_compare_fusion.5), kind=kOutput, calls=%fused_computation.80 | convolution fusion | flops 1003672960 | bytes 4861752 | tf_op jit(solution)/shard_map/kab,kz->zab/dot_general | solution.py:59
  463.6 6.5 %copy.38 = bf16[344,22,129]{2,1,0:T(8,128)(2,1)} copy(bf16[344,22,129]{0,2,1:T(8,128)(2,1)} %convolution_convert_fusion.3) | data formatting | bytes 3905088 | tf_op jit(solution)/shard_map/convert_element_type | solution.py:99
  470.2 9.3 %reshape.103 = bf16[4,2,122034]{2,1,0:T(2,128)(2,1)} reshape(bf16[344,22,129]{2,1,0:T(8,128)(2,1)} %copy.38) | data formatting | bytes 3905088
  479.5 4.9 all-to-all-start.3
  484.5 0.1 dynamic-slice_multiply_fusion
  484.6 0.1 dynamic-slice_multiply_fusion.1
  484.6 0.1 broadcast_add_fusion
  484.7 8.1 %reshape.102 = bf16[344,22,129]{2,1,0:T(8,128)(2,1)} reshape(bf16[4,2,122034]{2,1,0:T(2,128)(2,1)S(1)} %all-to-all-done.7) | data formatting | bytes 3905088
  492.8 7.2 %copy.52 = bf16[4,86,22,129]{1,3,0,2:T(8,128)(2,1)} copy(bf16[4,86,22,129]{3,2,1,0:T(8,128)(2,1)} %bitcast.141) | data formatting | bytes 3905088 | tf_op jit(solution)/shard_map/all_to_all | solution.py:103
  500.0 5.5 all_to_all.135
  505.5 3.9 all-to-all-done.3
  509.4 8.9 %reshape.104 = bf16[344,22,129]{2,1,0:T(8,128)(2,1)} reshape(bf16[4,2,122034]{2,1,0:T(2,128)(2,1)} %all-to-all-done.3) | data formatting | bytes 3905088
  518.3 7.2 %copy.39 = bf16[4,86,22,129]{1,3,0,2:T(8,128)(2,1)} copy(bf16[4,86,22,129]{3,2,1,0:T(8,128)(2,1)} %bitcast.142) | data formatting | bytes 3905088 | tf_op jit(solution)/shard_map/all_to_all | solution.py:102
  525.5 5.9 %all_to_all.119 = bf16[86,22,516]{0,2,1:T(8,128)(2,1)} reshape(bf16[86,22,4,129]{0,3,2,1:T(8,128)(2,1)} %bitcast.144) | data formatting | bytes 3905088 | tf_op jit(solution)/shard_map/all_to_all | solution.py:102
  531.4 0.0 copy-start.3
  531.4 14.5 %fusion.51 = f32[86,22,513]{2,0,1:T(8,128)} fusion(bf16[86,22,516]{0,2,1:T(8,128)(2,1)} %all_to_all.135, f32[513]{0:T(1024)S(1)} %get-tuple-element.5, f32[513]{0:T(1024)S(1)} %get-tuple-element.6), kind=kOutput, calls=%fused_computation.59 | convolution fusion | flops 2002107648 | bytes 5851312 | tf_op jit(solution)/shard_map/abk,kz->abz/dot_general | solution.py:59
  546.0 15.2 %fusion.43 = f32[86,22,513]{2,0,1:T(8,128)} fusion(bf16[86,22,513]{2,0,1:T(8,128)(2,1)} %param.5, bf16[86,22,516]{0,2,1:T(8,128)(2,1)} %all_to_all.119, bf16[513,513]{1,0:T(8,128)(2,1)S(1)} %copy-done.3, f32[513]{0:T(1024)S(1)} %get-tuple-element.6), kind=kOutput, calls=%fused_computation.53 | convolution fusion | flops 2000282496 | bytes 8449912 | tf_op jit(solution)/shard_map/abk,kz->abz/dot_general | solution.py:59
  561.2 9.7 %fusion.45 = f32[86,22,513]{2,0,1:T(8,128)} fusion(bf16[86,22,513]{2,0,1:T(8,128)(2,1)} %param.5, f32[86,22,513]{2,0,1:T(8,128)} %fusion.51, f32[86,22,513]{2,0,1:T(8,128)} %fusion.43, f32[86,22]{0,1:T(8,128)S(1)} %broadcast_add_fusion, f32[513]{0:T(1024)S(1)} %neg.4, bf16[513,513]{1,0:T(8,128)(2,1)S(1)} %copy-done.4, bf16[513,513]{1,0:T(8,128)(2,1)S(1)} %copy-done.3), kind=kOutput, calls=%fused_computation.54 | convolution fusion | flops 2001369088 | bytes 14650640 | tf_op jit(solution)/shard_map/abk,kz->abz/dot_general | solution.py:59
  570.9 8.7 %fusion.47 = f32[86,22,513]{2,0,1:T(8,128)} fusion(f32[86,22,513]{2,0,1:T(8,128)} %fusion.45, f32[86,22]{0,1:T(8,128)S(1)} %broadcast_add_fusion, f32[513]{0:T(1024)S(1)} %neg.4, bf16[513,513]{1,0:T(8,128)(2,1)S(1)} %copy-done.4, bf16[513,513]{1,0:T(8,128)(2,1)S(1)} %copy-done.3), kind=kOutput, calls=%fused_computation.55 | convolution fusion | flops 1996515968 | bytes 8827064 | tf_op jit(solution)/shard_map/abk,kz->abz/dot_general | solution.py:59
  579.5 7.4 %fusion.57 = f32[86,22,513]{2,0,1:T(8,128)} fusion(f32[86,22,513]{2,0,1:T(8,128)} %fusion.47, f32[86,22]{0,1:T(8,128)S(1)} %broadcast_add_fusion, f32[513]{0:T(1024)S(1)} %neg.4, bf16[513,513]{1,0:T(8,128)(2,1)S(1)} %copy-done.4), kind=kOutput, calls=%fused_computation.67 | convolution fusion | flops 999713856 | bytes 8300726 | tf_op jit(solution)/shard_map/abk,kz->abz/dot_general | solution.py:59
  (21 shorter events, 0.1 us)
Async XLA Ops:
  0.0 26.9 %copy-start = (bf16[86,22,513]{2,0,1:T(8,128)(2,1)S(1)}, bf16[86,22,513]{2,0,1:T(8,128)(2,1)}, u32[]{:S(2)}) copy-start(bf16[86,22,513]{2,0,1:T(8,128)(2,1)} %param.6) | copy-start | bytes 5823580
  20.9 44.0 %all-to-all-start = ((bf16[86,22,516]{0,1,2:T(8,128)(2,1)}), bf16[86,22,516]{0,1,2:T(8,128)(2,1)}, u32[]{:S(2)}, u32[]{:S(2)}) async-start(bf16[86,22,516]{0,1,2:T(8,128)(2,1)} %pad.7.clone), calls=%async_computation | async-start | bytes 6340608 | tf_op jit(solution)/shard_map/all_to_all | solution.py:83
  64.9 43.6 %all-to-all-start.4 = ((bf16[86,22,516]{0,1,2:T(8,128)(2,1)}), bf16[86,22,516]{0,1,2:T(8,128)(2,1)}, u32[]{:S(2)}, u32[]{:S(2)}) async-start(bf16[86,22,516]{0,1,2:T(8,128)(2,1)} %pad.8.clone), calls=%async_computation.4 | async-start | bytes 6340608 | tf_op jit(solution)/shard_map/all_to_all | solution.py:84
  108.5 45.7 %all-to-all-start.1 = ((bf16[32,2,22704]{2,1,0:T(2,128)(2,1)}), bf16[32,2,22704]{2,1,0:T(2,128)(2,1)}, u32[]{:S(2)}, u32[]{:S(2)}) async-start(bf16[32,2,22704]{2,1,0:T(2,128)(2,1)} %reshape.97), calls=%async_computation.1 | async-start | bytes 5832704 | tf_op jit(solution)/shard_map/all_to_all | solution.py:89
  154.2 60.8 %all-to-all-start.5 = ((bf16[32,2,22704]{2,1,0:T(2,128)(2,1)}), bf16[32,2,22704]{2,1,0:T(2,128)(2,1)}, u32[]{:S(2)}, u32[]{:S(2)}) async-start(bf16[32,2,22704]{2,1,0:T(2,128)(2,1)} %reshape.99), calls=%async_computation.5 | async-start | bytes 5832704 | tf_op jit(solution)/shard_map/all_to_all | solution.py:90
  273.1 84.3 %all-to-all-start.6 = ((bf16[16,704,129]{2,0,1:T(8,128)(2,1)}), bf16[16,704,129]{2,0,1:T(8,128)(2,1)}, u32[]{:S(2)}, u32[]{:S(2)}) async-start(bf16[16,704,129]{2,0,1:T(8,128)(2,1)} %copy.48), calls=%async_computation.6 | async-start | bytes 11534336 | tf_op jit(solution)/shard_map/all_to_all | solution.py:97
  357.4 83.9 %all-to-all-start.2 = ((bf16[16,704,129]{2,0,1:T(8,128)(2,1)}), bf16[16,704,129]{2,0,1:T(8,128)(2,1)}, u32[]{:S(2)}, u32[]{:S(2)}) async-start(bf16[16,704,129]{2,0,1:T(8,128)(2,1)} %copy.35), calls=%async_computation.2 | async-start | bytes 11534336 | tf_op jit(solution)/shard_map/all_to_all | solution.py:96
  441.2 38.3 %all-to-all-start.7 = ((bf16[4,2,122034]{2,1,0:T(2,128)(2,1)}), bf16[4,2,122034]{2,1,0:T(2,128)(2,1)S(1)}, u32[]{:S(2)}, u32[]{:S(2)}) async-start(bf16[4,2,122034]{2,1,0:T(2,128)(2,1)} %reshape.101), calls=%async_computation.7 | async-start | bytes 3907584 | tf_op jit(solution)/shard_map/all_to_all | solution.py:103
  479.5 4.9 copy-start.2
  479.5 29.8 %all-to-all-start.3 = ((bf16[4,2,122034]{2,1,0:T(2,128)(2,1)}), bf16[4,2,122034]{2,1,0:T(2,128)(2,1)}, u32[]{:S(2)}, u32[]{:S(2)}) async-start(bf16[4,2,122034]{2,1,0:T(2,128)(2,1)} %reshape.103), calls=%async_computation.3 | async-start | bytes 3907584 | tf_op jit(solution)/shard_map/all_to_all | solution.py:102
  531.4 14.6 %copy-start.3 = (bf16[513,513]{1,0:T(8,128)(2,1)S(1)}, bf16[513,513]{1,0:T(8,128)(2,1)}, u32[]{:S(2)}) copy-start(bf16[513,513]{1,0:T(8,128)(2,1)} %param.8) | copy-start | bytes 1579018
  546.0 15.2 %copy-start.4 = (bf16[513,513]{1,0:T(8,128)(2,1)S(1)}, bf16[513,513]{1,0:T(8,128)(2,1)}, u32[]{:S(2)}) copy-start(bf16[513,513]{1,0:T(8,128)(2,1)} %param.7) | copy-start | bytes 1579018
  579.5 7.4 %copy-start.1 = (bf16[86,22,513]{2,0,1:T(8,128)(2,1)S(1)}, bf16[86,22,513]{2,0,1:T(8,128)(2,1)}, u32[]{:S(2)}) copy-start(bf16[86,22,513]{2,0,1:T(8,128)(2,1)} %param.6) | copy-start | bytes 5823580
where the time goes:
time: 597 us; the launch traced here: 587 us
  local copies, waits for them, and re-layouts  218 us (37%)
  matrix products  167 us (28%)
  waiting for transfers between devices  125 us (21%)
  starting transfers between devices  59.1 us (10%)
  other arithmetic  17.9 us (3%)
    dot_general x14, matrix products, along(): jnp.einsum(forms[which], values, table, preferred_element_type=jnp.float32)  167 us
    unnamed x20, local copies, waits for them, and re-layouts  98.9 us
    all_to_all x1, waiting for transfers between devices, per_device(): lax.all_to_all(cube_stream, 'nx', split_axis=1, concat_axis=0, tiled=True)  54.2 us
    all_to_all x1, waiting for transfers between devices, per_device(): lax.all_to_all(flux_stream, 'nx', split_axis=1, concat_axis=0, tiled=True)  46.3 us
    all_to_all x1, waiting for transfers between devices, per_device(): lax.all_to_all(phi_padded, 'nz', split_axis=2, concat_axis=0, tiled=True)  18.8 us
    dot_general x2, other arithmetic, along(): jnp.einsum(forms[which], values, table, preferred_element_type=jnp.float32)  17.6 us
    all_to_all x2, local copies, waits for them, and re-layouts, per_device(): lax.all_to_all(cube_span, 'nz', split_axis=0, concat_axis=2, tiled=True)  13.1 us
    all_to_all x2, local copies, waits for them, and re-layouts, per_device(): lax.all_to_all(flux_span, 'nz', split_axis=0, concat_axis=2, tiled=True)  12.7 us
  transfers between devices with their start and end apart: 8, of which 5 were waited for; matrix products, arithmetic and copies ran while one was open for 39% of the time, Pallas kernels for 0%

commit v1 on v0

v1 whole, which is shorter than its diff:
```python
import math

import jax
import jax.numpy as jnp
import ml_dtypes
import numpy as np
from jax import lax
from jax.experimental import pallas as pl
from jax.experimental.pallas import tpu as pltpu
from jax.sharding import PartitionSpec as P

NX = 1024
NZ = 512

mobility = 1.0
capillary = 0.2
screen_low = 4.0
screen_high = 20.0
time_step = 1.0 / (screen_low * screen_high * mobility * capillary)
stabilizer = capillary * (screen_low + screen_high)

PLANES = 4
HALVES = 2
WINDOW = 88
LANES = 1024
TILE = 128
BF = ml_dtypes.bfloat16
F32 = jnp.float32
BF16 = jnp.bfloat16


def fourier_tables(mode_count, point_count):
    half_count = mode_count // 2
    mode_index = np.arange(mode_count)
    wave_index = np.where(mode_index < half_count, mode_index, mode_index - half_count + 1)
    phase_steps = wave_index[:, None] * np.arange(point_count)[None, :] % point_count
    angles = phase_steps * (2.0 * math.pi / point_count)
    basis = np.where((mode_index < half_count)[:, None], np.cos(angles), np.sin(angles))
    factor = math.sqrt(2.0 / mode_count)
    weights = np.where(mode_index == 0, 1.0, 2.0) / (point_count * factor)
    wavenumber = 2.0 * wave_index / half_count
    return (
        (factor * basis).astype(np.float32).astype(BF),
        (basis.T * weights[None, :]).astype(np.float32).astype(BF),
        wavenumber.astype(np.float32),
    )


def chebyshev_tables(count):
    index = np.arange(count)
    phase_steps = index[:, None] * index[None, :] % (2 * (count - 1))
    cosines = np.cos(phase_steps * (math.pi / (count - 1)))
    factor = math.sqrt(2.0 / count)
    ends = np.where((index == 0) | (index == count - 1), 2.0, 1.0)
    analysis = cosines.T * (2.0 / ((count - 1) * factor)) / (ends[:, None] * ends[None, :])
    upper, lower = index[:, None], index[None, :]
    deriv = np.where((upper > lower) & ((upper + lower) % 2 == 1), 2.0 * upper / ends[None, :], 0.0)
    as_bf = lambda t: t.astype(np.float32).astype(BF)
    return as_bf(factor * cosines), as_bf(analysis), as_bf(deriv)


def dot(left, right):
    return jnp.dot(left, right, preferred_element_type=F32)


def dot_nt(left, right):
    return lax.dot_general(left, right, (((1,), (1,)), ((), ())), preferred_element_type=F32)


def dot_tn(left, right):
    return lax.dot_general(left, right, (((0,), (0,)), ((), ())), preferred_element_type=F32)


def rows_of(shape, axis):
    return lax.broadcasted_iota(jnp.int32, shape, axis)


MESH = pl.DeviceIdType.MESH
DEVICES = 128
BLOCK = 256
WIDE = 512


class Place:
    def __init__(self):
        self.a, self.b = lax.axis_index("nz"), lax.axis_index("nx")
        self.me = self.a * 32 + self.b
        self.core = lax.rem(self.a, 2)
        self.y = (self.a // 2) * 2 + lax.rem(self.b // 4, 2)
        self.z, self.x = self.b // 8, lax.rem(self.b, 4)

    def at(self, dz, dy, dx, dc):
        z, y, x = lax.rem(self.z + dz, 4), lax.rem(self.y + dy, 4), lax.rem(self.x + dx, 4)
        core = lax.rem(self.core + dc, 2)
        return (y // 2) * 2 + core, z * 8 + lax.rem(y, 2) * 4 + x

    def partner(self, i):
        u, v, w, dc = lax.rem(i, 4), lax.rem(i // 4, 4), lax.rem(i // 16, 4), i // 64
        sign = 1 - 2 * self.core
        turn = lambda d: lax.rem(4 + sign * lax.rem(d, 4), 4)
        return self.at(turn(3 * u + 2 * v + w), turn(u + v), turn(u), dc)


def transfer(src, dst, sems, device):
    return pltpu.make_async_remote_copy(
        src_ref=src, dst_ref=dst, send_sem=sems.at[0], recv_sem=sems.at[1], device_id=device, device_id_type=MESH
    )


def scatter(place, src, dst, sems, own_sem):
    own = pltpu.make_async_copy(src.at[place.me], dst.at[place.me], own_sem)
    own.start()

    def send(i, carry):
        a, b = place.partner(i)
        transfer(src.at[a * 32 + b], dst.at[place.me], sems, (a, b)).start()
        return carry

    lax.fori_loop(1, DEVICES, send, 0)
    own.wait()


def all_chunks(place, src, dst, sems):
    others = pl.ds(0, DEVICES - 1)
    return transfer(src.at[others], dst.at[others], sems, place.at(0, 0, 1, 0))


def stage_modes(modes_ref, stage_ref, h):
    streams, spans, _ = modes_ref.shape
    half = streams // HALVES
    for k in range(half):
        stage_ref[pl.ds(k * WINDOW, spans), :] = modes_ref[h * half + k].astype(F32)


def synth_y(h, stage_ref, table, work_ref, flip_ref):
    cheb = stage_ref.shape[1]
    points = table.shape[0] if flip_ref is None else table.shape[0] // 2

    def columns(i, carry):
        lines = dot_nt(table, stage_ref[pl.ds(pl.multiple_of(i * BLOCK, BLOCK), BLOCK), :].astype(BF16))
        lane = pl.ds(pl.multiple_of(lax.rem(i, 2) * BLOCK, BLOCK), BLOCK)
        work_ref[2 * h + i // 2, 0:points, lane] = lines[0:points]
        if flip_ref is not None:
            flip_ref[h, :, pl.ds(pl.multiple_of(i * BLOCK, BLOCK), BLOCK)] = lines[points : points + cheb].astype(BF16)
        return carry

    lax.fori_loop(0, LANES // BLOCK, columns, 0)


def pack_chunks(work_ref, chunk_ref):
    rows = DEVICES * PLANES

    def pack(i, carry):
        lane = pl.ds(pl.multiple_of(lax.rem(i, 4) * TILE, TILE), TILE)
        low = work_ref[i // 4, 0:rows, lane].reshape(rows // 8, 8, TILE)
        high = work_ref[2 + i // 4, 0:rows, lane].reshape(rows // 8, 8, TILE)
        upper = rows_of(low.shape, 1) < 4
        even = jnp.where(upper, low, pltpu.roll(high, 4, 1))
        odd = jnp.where(upper, pltpu.roll(low, 4, 1), high)
        both = jnp.stack([even, odd], axis=1).reshape(DEVICES, 8, TILE)
        chunk_ref[:, :, pl.ds(pl.multiple_of(i * TILE, TILE), TILE)] = both.astype(BF16)
        return carry

    lax.fori_loop(0, LANES // TILE, pack, 0)


def unpack_rows(chunk_ref, h, at):
    chunk = chunk_ref[:, :, at].astype(F32)
    width = chunk.shape[2]
    pairs = chunk.reshape(DEVICES // 2, 2, 8, width)
    even, odd = pairs[:, 0], pairs[:, 1]
    upper = rows_of(even.shape, 1) < 4
    if h == 0:
        rows = jnp.where(upper, even, pltpu.roll(odd, 4, 1))
    else:
        rows = jnp.where(upper, pltpu.roll(even, 4, 1), odd)
    return rows.reshape(DEVICES * PLANES, width).astype(BF16)


def window_place(k):
    off = k * WINDOW
    first, shift = off // TILE, lax.rem(off, TILE)
    at = pl.ds(pl.multiple_of(first * TILE, TILE), TILE)
    after = pl.ds(pl.multiple_of((first + 1) * TILE, TILE), TILE)
    return shift, at, after


def synth_z(chunk_ref, table_ref, plane_ref, stage_ref, planes):
    group = DEVICES // 4
    rows = group * 8
    part = rows // PLANES

    def window(k, carry):
        shift, at, after = window_place(k)
        parts = []
        for a in range(4):
            own = pl.ds(a * group, group)
            left = chunk_ref[own, :, at].astype(F32).reshape(rows, TILE)
            right = chunk_ref[own, :, after].astype(F32).reshape(rows, TILE)
            mixed = jnp.where(rows_of(left.shape, 1) >= shift, left, right)
            parts.append(pltpu.roll(mixed, lax.rem(TILE - shift, TILE), 1).astype(BF16))
        points = dot(jnp.concatenate(parts, axis=1), table_ref[...])
        for c in range(NZ // TILE):
            stage_ref[c] = points[:, c * TILE : (c + 1) * TILE]
            for p in range(planes):
                plane_ref[p, pl.ds(pl.multiple_of(k * part, part), part), c * TILE : (c + 1) * TILE] = stage_ref[
                    c, pl.ds(p, part, stride=PLANES), :
                ].astype(BF16)
        return carry

    lax.fori_loop(0, 11, window, 0)


def analyse_z(stream_ref, table_ref, chunk_ref):
    group = DEVICES // 4

    def window(k, carry):
        shift, at, after = window_place(k)
        points = jnp.concatenate([stream_ref[k, c].astype(BF16) for c in range(NZ // TILE)], axis=1)
        lines = dot(points, table_ref[...])
        for a in range(4):
            own = pl.ds(a * group, group)
            moved = pltpu.roll(lines[:, a * TILE : (a + 1) * TILE], shift, 1).reshape(group, 8, TILE)
            keep = rows_of(moved.shape, 2) >= shift
            chunk_ref[own, :, at] = jnp.where(keep, moved, chunk_ref[own, :, at].astype(F32)).astype(BF16)
            chunk_ref[own, :, after] = moved.astype(BF16)
        return carry

    lax.fori_loop(0, 11, window, 0)


def keep_lines(stream_ref, lines, p, c):
    part = lines.shape[0] // 11
    for k in range(11):
        for t in range(BLOCK // TILE):
            stream_ref[k, c * (BLOCK // TILE) + t, pl.ds(p, part, stride=PLANES), :] = lines[
                k * part : (k + 1) * part, t * TILE : (t + 1) * TILE
            ]


def column_loop(body):
    def step(c, carry):
        body(c, pl.ds(pl.multiple_of(c * BLOCK, BLOCK), BLOCK))
        return carry

    lax.fori_loop(0, NZ // BLOCK, step, 0)


def gather_last(place, last_ref, sems):
    me, b = place.me, place.b
    own = pl.ds(me, 1)
    four, eight, all_x = pl.ds(place.a * 32 + (b // 4) * 4, 4), pl.ds(place.a * 32 + (b // 8) * 8, 8), pl.ds(place.a * 32, 32)
    other = lax.rem(place.a + 2, 4), b
    pair = place.at(0, 0, 0, 1)
    lower = pl.ds(place.core * 32, 32)
    upper = pl.ds(place.core * 32 + 64, 32)
    beside = place.a, (b // 8) * 8 + lax.rem(b // 4 + 1, 2) * 4 + place.x
    return [
        ([(own, place.at(0, 0, d, 0)) for d in (1, 2, 3)], 3),
        ([(four, beside)], 4),
        ([(eight, place.at(d, 0, 0, 0)) for d in (1, 2, 3)], 24),
        ([(all_x, other)], 32),
        ([(lower, pair), (upper, pair)], 64),
    ]


def kernel(
    phi_hbm, vel_hbm, both_hbm, synth_z_hbm, synth_x_hbm, analy_x_hbm, analy_z_hbm, analy_y_hbm, deriv_hbm, dual_hbm, basis_hbm,
    basis_t_hbm, own_x_ref, squares_ref, rates_ref, edge_ref, out_ref,
    modes_ref, both_ref, synth_z_ref, synth_x_ref, analy_x_ref, analy_z_ref, analy_y_ref, deriv_ref, dual_ref, basis_ref,
    basis_t_ref, stage_ref, work_ref, flip_ref, plane_ref, points_ref, stream_ref, slab_ref, last_ref, small_ref, extra_ref,
    phi_send, vel_send, phi_recv, vel_recv, cube_recv, flux_recv,
    table_sems, modes_sem, own_sem, phi_sems, vel_sems, cube_sems, flux_sems, last_sems,
):
    place = Place()
    cheb = dual_ref.shape[0]
    streams, spans, _ = out_ref.shape
    half = streams // HALVES

    modes_copy = pltpu.make_async_copy(phi_hbm, modes_ref, modes_sem)
    modes_copy.start()
    moves = {}
    pairs = dict(
        both=(both_hbm, both_ref), synth_z=(synth_z_hbm, synth_z_ref), synth_x=(synth_x_hbm, synth_x_ref),
        analy_x=(analy_x_hbm, analy_x_ref), analy_z=(analy_z_hbm, analy_z_ref), analy_y=(analy_y_hbm, analy_y_ref),
        deriv=(deriv_hbm, deriv_ref), dual=(dual_hbm, dual_ref), basis=(basis_hbm, basis_ref), basis_t=(basis_t_hbm, basis_t_ref),
    )
    for i, (name, (src, dst)) in enumerate(pairs.items()):
        moves[name] = pltpu.make_async_copy(src, dst, table_sems.at[i])
        moves[name].start()

    barrier = pltpu.get_barrier_semaphore()

    def greet(i, carry):
        pl.semaphore_signal(barrier, inc=1, device_id=place.partner(i), device_id_type=MESH)
        return carry

    lax.fori_loop(1, DEVICES, greet, 0)

    stage_ref[...] = jnp.zeros_like(stage_ref)
    modes_copy.wait()
    stage_modes(modes_ref, stage_ref, 0)
    moves["both"].wait()
    synth_y(0, stage_ref, both_ref[...], work_ref, flip_ref)
    stage_modes(modes_ref, stage_ref, 1)
    vel_copy = pltpu.make_async_copy(vel_hbm, modes_ref, modes_sem)
    vel_copy.start()
    synth_y(1, stage_ref, both_ref[...], work_ref, flip_ref)
    pack_chunks(work_ref, phi_send)
    pl.semaphore_wait(barrier, DEVICES - 1)
    scatter(place, phi_send, phi_recv, phi_sems, own_sem)
    for h in range(HALVES):
        for t in range(2):
            slab_ref[pl.ds(h * 4 + t * 2, 1), :] = work_ref[2 * h + t, pl.ds(cheb - 1, 1), :]

    vel_copy.wait()
    points_rows = both_ref.shape[0] // 2
    for h in range(HALVES):
        stage_modes(modes_ref, stage_ref, h)
        synth_y(h, stage_ref, both_ref[0:points_rows, :], work_ref, None)
    pack_chunks(work_ref, vel_send)
    for h in range(HALVES):
        for t in range(2):
            slab_ref[pl.ds(h * 4 + t * 2 + 1, 1), :] = work_ref[2 * h + t, pl.ds(cheb - 1, 1), :]
    last_ref[pl.ds(place.me, 1)] = slab_ref[...].astype(BF16).reshape(1, 8, WIDE)
    stages = gather_last(place, last_ref, last_sems)

    def gather_step(i):
        copies, total = stages[i]
        for rows, device in copies:
            transfer(last_ref.at[rows], last_ref.at[rows], last_sems.at[i], device).start()

    def gather_wait(i):
        copies, total = stages[i]
        block = pl.ds(0, total)
        done = transfer(last_ref.at[block], last_ref.at[block], last_sems.at[i], copies[0][1])
        done.wait_send()
        done.wait_recv()

    gather_step(0)
    scatter(place, vel_send, vel_recv, vel_sems, own_sem)
    for i in range(1, len(stages)):
        gather_wait(i - 1)
        gather_step(i)

    moves["synth_z"].wait()
    moves["synth_x"].wait()
    all_chunks(place, phi_send, phi_recv, phi_sems).wait_recv()
    synth_z(phi_recv, synth_z_ref, plane_ref, points_ref, PLANES)
    for p in range(PLANES):

        def phi_columns(c, at, p=p):
            work_ref[p, :, at] = dot(synth_x_ref[...], plane_ref[p, :, at])

        column_loop(phi_columns)

    all_chunks(place, vel_send, vel_recv, vel_sems).wait_recv()
    synth_z(vel_recv, synth_z_ref, plane_ref, points_ref, PLANES)
    moves["analy_x"].wait()
    moves["analy_z"].wait()
    for p in range(PLANES):

        def cube_columns(c, at, p=p):
            vel = dot(synth_x_ref[...], plane_ref[p, :, at])
            phi = work_ref[p, :, at]
            work_ref[p, :, at] = vel * phi
            keep_lines(stream_ref, dot(analy_x_ref[...], (phi * phi * phi).astype(BF16)), p, c)

        column_loop(cube_columns)

    all_chunks(place, phi_send, phi_recv, phi_sems).wait_send()
    phi_send[...] = jnp.zeros_like(phi_send)
    analyse_z(stream_ref, analy_z_ref, phi_send)
    scatter(place, phi_send, cube_recv, cube_sems, own_sem)
    for p in range(PLANES):

        def flux_columns(c, at, p=p):
            keep_lines(stream_ref, dot(analy_x_ref[...], work_ref[p, :, at].astype(BF16)), p, c)

        column_loop(flux_columns)

    all_chunks(place, vel_send, vel_recv, vel_sems).wait_send()
    vel_send[...] = jnp.zeros_like(vel_send)
    analyse_z(stream_ref, analy_z_ref, vel_send)
    scatter(place, vel_send, flux_recv, flux_sems, own_sem)

    gather_wait(len(stages) - 1)

    def spread(i, carry):
        some = pl.ds(pl.multiple_of(i * 16, 16), 16)
        chunk = last_ref[some]
        phi_recv[some, :, 0:WIDE] = chunk
        phi_recv[some, :, WIDE:LANES] = pltpu.roll(chunk.astype(F32), 6, 1).astype(BF16)
        return carry

    lax.fori_loop(0, DEVICES // 16, spread, 0)
    synth_z(phi_recv, synth_z_ref, plane_ref, points_ref, 2)

    def last_columns(c, at):
        phi = dot(synth_x_ref[...], plane_ref[0, :, at])
        vel = dot(synth_x_ref[...], plane_ref[1, :, at])
        small_ref[0, :, at] = dot(own_x_ref[...], (phi * phi * phi).astype(BF16)).astype(BF16)
        small_ref[1, :, at] = dot(own_x_ref[...], (vel * phi).astype(BF16)).astype(BF16)

    column_loop(last_columns)
    own_z = analy_z_ref[:, pl.ds(pl.multiple_of(place.a * TILE, TILE), TILE)]
    lane = rows_of((1, TILE), 1)
    for g in range(2):
        lines = dot(small_ref[g], own_z).astype(BF16).astype(F32)
        for h in range(HALVES):
            for k in range(half):
                first, shift = divmod(k * WINDOW, TILE)
                row = h * half + k
                moved = lines[row : row + 1]
                moved = pltpu.roll(moved, shift, 1) if shift else moved
                here = slice(first * TILE, (first + 1) * TILE)
                if shift:
                    moved_in = jnp.where(lane >= shift, moved, extra_ref[g, h, 0:1, here])
                else:
                    moved_in = moved
                extra_ref[g, h, 0:1, here] = moved_in
                extra_ref[g, h, 0:1, (first + 1) * TILE : (first + 2) * TILE] = moved

    for name in ("analy_y", "deriv", "dual", "basis", "basis_t"):
        moves[name].wait()
    eig = -rates_ref[...]
    all_chunks(place, phi_send, cube_recv, cube_sems).wait_recv()
    for h in range(HALVES):

        def lap_columns(i, carry, h=h):
            at = pl.ds(pl.multiple_of(i * WIDE, WIDE), WIDE)
            phi = flip_ref[h, :, at].astype(F32)
            cube = dot(analy_y_ref[...], unpack_rows(cube_recv, h, at)) + edge_ref[...] * extra_ref[0, h, 0:1, at]
            source = (cube - (1.0 + stabilizer) * phi).astype(BF16)
            scaled = ((eig - squares_ref[h, :, at]) * dot(dual_ref[...], source)).astype(BF16)
            work_ref[2 * h + i, 0:cheb, :] = dot(basis_ref[...], scaled)
            return carry

        lax.fori_loop(0, LANES // WIDE, lap_columns, 0)
    all_chunks(place, vel_send, flux_recv, flux_sems).wait_recv()
    for h in range(HALVES):
        for i in range(LANES // WIDE):
            start = i * WIDE
            at = pl.ds(start, WIDE)
            squares = squares_ref[h, :, at]
            phi = flip_ref[h, :, at].astype(F32)
            flux = dot(analy_y_ref[...], unpack_rows(flux_recv, h, at)) + edge_ref[...] * extra_ref[1, h, 0:1, at]
            slope = dot(deriv_ref[...], flux.astype(BF16))
            lap = work_ref[2 * h + i, 0:cheb, :]
            forcing = (
                (phi / time_step + mobility * lap - 8.0 / (cheb - 1) * slope) / (capillary * mobility)
            ).astype(BF16)
            first = (dot(dual_ref[...], forcing) / (eig - squares - screen_low)).astype(BF16)
            middle = dot(basis_ref[...], first).astype(BF16)
            second = (dot(dual_ref[...], middle) / (eig - squares - screen_high)).astype(BF16)
            result = dot_tn(second, basis_t_ref[...])
            for k in range(half):
                low, high = max(k * WINDOW, start), min(k * WINDOW + spans, start + WIDE)
                if low < high:
                    out_ref[h * half + k, low - k * WINDOW : high - k * WINDOW, :] = result[low - start : high - start]
    all_chunks(place, phi_send, cube_recv, cube_sems).wait_send()
    all_chunks(place, vel_send, flux_recv, flux_sems).wait_send()


def per_device(phi_hat, vel_hat, helm_basis, helm_dual, helm_rates):
    span_count = lax.axis_size("nz")
    stream_count = lax.axis_size("nx")
    span_local, stream_local, cheb = phi_hat.shape
    half = stream_local // HALVES
    a, b = lax.axis_index("nz"), lax.axis_index("nx")

    s_x, a_x, wave_x = fourier_tables(stream_local * stream_count, NX)
    s_z, a_z, wave_z = fourier_tables(span_local * span_count, NZ)
    s_y, a_y, d_y = chebyshev_tables(cheb)

    pad = -cheb % 16
    points = np.pad(s_y.T, ((0, pad), (0, 0)))
    both = np.concatenate([points, np.pad(np.eye(cheb, dtype=np.float32).astype(BF), ((0, pad), (0, 0)))])
    order = np.arange(stream_local * stream_count).reshape(stream_count, HALVES, half).transpose(2, 0, 1).reshape(-1)
    synth_x = np.ascontiguousarray(s_x.T[:, order])
    analy_x = np.ascontiguousarray(a_x.T[order])
    own_all = np.pad(a_x.T.reshape(stream_count, stream_local, NX), ((0, 0), (0, 32 - stream_local), (0, 0)))
    synth_z = np.pad(s_z.reshape(span_count, span_local, NZ), ((0, 0), (0, TILE - span_local), (0, 0))).reshape(-1, NZ)
    analy_z = np.pad(a_z.reshape(NZ, span_count, span_local), ((0, 0), (0, 0), (0, TILE - span_local))).reshape(NZ, -1)

    wave_s = lax.dynamic_slice_in_dim(jnp.asarray(wave_x), b * stream_local, stream_local)
    wave_p = lax.dynamic_slice_in_dim(jnp.asarray(wave_z), a * span_local, span_local)
    squares = wave_s[:, None] * wave_s[:, None] + wave_p[None, :] * wave_p[None, :]
    squares = jnp.pad(squares, ((0, 0), (0, WINDOW - span_local))).reshape(HALVES, 1, half * WINDOW)
    squares = jnp.pad(squares, ((0, 0), (0, 0), (0, LANES - half * WINDOW)))

    large = [
        jnp.transpose(phi_hat, (1, 0, 2)), jnp.transpose(vel_hat, (1, 0, 2)), jnp.asarray(both), jnp.asarray(synth_z),
        jnp.asarray(synth_x), jnp.asarray(analy_x), jnp.asarray(analy_z), jnp.asarray(np.ascontiguousarray(a_y[: cheb - 1].T)),
        jnp.asarray(np.ascontiguousarray(d_y.T)), helm_dual, helm_basis, helm_basis.T,
    ]
    small = [
        lax.dynamic_index_in_dim(jnp.asarray(own_all), b, 0, keepdims=False), squares, helm_rates[:, None],
        jnp.asarray(a_y[cheb - 1 :].T.astype(np.float32)),
    ]
    modes_x = stream_local * stream_count
    chunk = pltpu.VMEM((DEVICES, 8, LANES), BF16)
    sems = pltpu.SemaphoreType.DMA((2,))
    result = pl.pallas_call(
        kernel,
        out_shape=jax.ShapeDtypeStruct((stream_local, span_local, cheb), F32),
        in_specs=[pl.BlockSpec(memory_space=pl.ANY)] * len(large) + [pl.BlockSpec(memory_space=pltpu.VMEM)] * len(small),
        out_specs=pl.BlockSpec(memory_space=pltpu.VMEM),
        scratch_shapes=[pltpu.VMEM(large[0].shape, BF16)]
        + [pltpu.VMEM(table.shape, BF16) for table in large[2:]]
        + [
            pltpu.VMEM((LANES, cheb), F32),
            pltpu.VMEM((PLANES, NX, NZ), F32),
            pltpu.VMEM((HALVES, cheb, LANES), BF16),
            pltpu.VMEM((PLANES, modes_x, NZ), BF16),
            pltpu.VMEM((NZ // TILE, 256, TILE), F32),
            pltpu.VMEM((11, NZ // TILE, 256, TILE), F32),
            pltpu.VMEM((8, WIDE), F32),
            pltpu.VMEM((DEVICES, 8, WIDE), BF16),
            pltpu.VMEM((2, 32, NZ), BF16),
            pltpu.VMEM((2, HALVES, 8, LANES), F32),
        ]
        + [chunk] * 6
        + [
            pltpu.SemaphoreType.DMA((len(large) - 2,)), pltpu.SemaphoreType.DMA, pltpu.SemaphoreType.DMA,
            sems, sems, sems, sems, pltpu.SemaphoreType.DMA((5, 2)),
        ],
        compiler_params=pltpu.CompilerParams(collective_id=0, has_side_effects=True, vmem_limit_bytes=60 << 20),
    )(*large, *small)
    return jnp.transpose(result, (1, 0, 2))


def solution(mesh):
    placed = (P("nz", "nx", None), P("nz", "nx", None), P(), P(), P())
    return jax.shard_map(
        per_device, mesh=mesh, in_specs=placed, out_specs=P("nz", "nx", None), check_vma=False
    )
```

time: 597 us -> 182 us (0.30); the launches traced: 587 us -> 181 us
  local copies, waits for them, and re-layouts: 218 us -> 10.9 us
  Pallas kernels: 0 us -> 169 us
  matrix products: 167 us -> 0 us
  waiting for transfers between devices: 125 us -> 0 us
  starting transfers between devices: 59.1 us -> 0 us
  other arithmetic: 17.9 us -> 1.59 us
    pallas_call x0 -> x1, Pallas kernels: none -> 169 us  [per_device(): pl.pallas_call(kernel, out_shape=jax.ShapeDtypeStruct((stream_local, span...]
    dot_general x14 -> x0, matrix products: 167 us -> none  [along(): jnp.einsum(forms[which], values, table, preferred_element_type=jnp.float32)]
    all_to_all x8 -> x0, waiting for transfers between devices: 125 us -> none  [the longest x1 54.2 us: per_device(): lax.all_to_all(cube_stream, 'nx', split_axis=1, concat_axis=0, tiled=True)]
    unnamed x20 -> x2, local copies, waits for them, and re-layouts: 98.9 us -> 7.19 us
    all_to_all x12 -> x0, local copies, waits for them, and re-layouts: 63.4 us -> none  [the longest x2 13.1 us: per_device(): lax.all_to_all(cube_span, 'nz', split_axis=0, concat_axis=2, tiled=True)]
    all_to_all x8 -> x0, starting transfers between devices: 59.1 us -> none  [the longest x1 9.31 us: per_device(): lax.all_to_all(phi_span, 'nx', split_axis=0, concat_axis=1, tiled=True)]
    convert_element_type x6 -> x0, local copies, waits for them, and re-layouts: 47.3 us -> none  [the longest x1 9.08 us: per_device(): phi_span = along(pieces[0], synth_z, 0).astype(jnp.bfloat16)]
    dot_general x2 -> x0, other arithmetic: 17.6 us -> none  [along(): jnp.einsum(forms[which], values, table, preferred_element_type=jnp.float32)]
  transfers between devices with their start and end apart: 8 -> 0, of which waited for: 5 -> 0; matrix products, arithmetic and copies ran while one was open for 39% -> 0% of each run, Pallas kernels for 0% -> 0%
where the time goes in v1:
time: 182 us; the launch traced here: 181 us
  Pallas kernels  169 us (93%)
  local copies, waits for them, and re-layouts  10.9 us (6%)
    pallas_call x1, Pallas kernels, per_device(): pl.pallas_call(kernel, out_shape=jax.ShapeDtypeStruct((stream_local, span...  169 us
    unnamed x2, local copies, waits for them, and re-layouts  7.19 us

profile of v1, /device:TPU:1, one launch (start us, length us, event | category | flops | bytes accessed | tf_op | source)
XLA Modules:
  0.0 181.4 jit_solution(2885014147968286548)
XLA Ops:
  0.0 0.8 dynamic-slice_multiply_fusion
  0.8 0.8 dynamic-slice_multiply_fusion.1
  1.5 0.1 broadcast_add_fusion
  1.6 0.1 reshape.7
  1.7 0.6 pad.9.squares_ref
  2.3 1.5 dynamic-slice_bitcast_fusion.own_x_ref
  3.8 1.5 broadcast_in_dim.3.rates_ref
  5.3 2.2 %copy.18 = bf16[513,513]{0,1:T(8,128)(2,1)} copy(bf16[513,513]{1,0:T(8,128)(2,1)} %basis_hbm.1) | data formatting | bytes 1052676 | tf_op args[2]
  7.5 168.9 %shard_map.154 = f32[22,86,513]{2,1,0:T(8,128)} custom-call(bf16[22,86,513]{2,1,0:T(8,128)(2,1)} %bitcast.8, bf16[22,86,513]{2,1,0:T(8,128)(2,1)} %bitcast.9, bf16[1056,513]{1,0:T(8,128)(2,1)} %constant.50.clone.both_hbm, bf16[512,512]{1,0:T(8,128)(2,1)} %constant.51.clone.synth_z_hbm, bf16[1024,704]{1,0:T(8,128)(2,1)} %constant.52.clone.synth_x_hbm, ...), custom_call_target="tpu_custom_call" | custom-call | tf_op jit(solution)/shard_map/pallas_call | solution.py:504
  176.4 5.0 %copy.21 = f32[86,22,513]{2,0,1:T(8,128)} copy(f32[86,22,513]{2,0,1:T(8,128)} %bitcast.6) | data formatting | bytes 7764768
  (1 shorter events, 0.0 us)

commit v2 on v1

v2 whole, which is shorter than its diff:
```python
import math

import jax
import jax.numpy as jnp
import ml_dtypes
import numpy as np
from jax import lax
from jax.experimental import pallas as pl
from jax.experimental.pallas import tpu as pltpu
from jax.sharding import PartitionSpec as P

NX = 1024
NZ = 512

mobility = 1.0
capillary = 0.2
screen_low = 4.0
screen_high = 20.0
time_step = 1.0 / (screen_low * screen_high * mobility * capillary)
stabilizer = capillary * (screen_low + screen_high)

PLANES = 4
HALVES = 2
WINDOW = 88
LANES = 1024
TILE = 128
BF = ml_dtypes.bfloat16
F32 = jnp.float32
BF16 = jnp.bfloat16


def fourier_tables(mode_count, point_count):
    half_count = mode_count // 2
    mode_index = np.arange(mode_count)
    wave_index = np.where(mode_index < half_count, mode_index, mode_index - half_count + 1)
    phase_steps = wave_index[:, None] * np.arange(point_count)[None, :] % point_count
    angles = phase_steps * (2.0 * math.pi / point_count)
    basis = np.where((mode_index < half_count)[:, None], np.cos(angles), np.sin(angles))
    factor = math.sqrt(2.0 / mode_count)
    weights = np.where(mode_index == 0, 1.0, 2.0) / (point_count * factor)
    return (
        (factor * basis).astype(np.float32).astype(BF),
        (basis.T * weights[None, :]).astype(np.float32).astype(BF),
    )


def chebyshev_tables(count):
    index = np.arange(count)
    phase_steps = index[:, None] * index[None, :] % (2 * (count - 1))
    cosines = np.cos(phase_steps * (math.pi / (count - 1)))
    factor = math.sqrt(2.0 / count)
    ends = np.where((index == 0) | (index == count - 1), 2.0, 1.0)
    analysis = cosines.T * (2.0 / ((count - 1) * factor)) / (ends[:, None] * ends[None, :])
    upper, lower = index[:, None], index[None, :]
    deriv = np.where((upper > lower) & ((upper + lower) % 2 == 1), 2.0 * upper / ends[None, :], 0.0)
    as_bf = lambda t: t.astype(np.float32).astype(BF)
    return as_bf(factor * cosines), as_bf(analysis), as_bf(deriv)


def dot(left, right):
    return jnp.dot(left, right, preferred_element_type=F32)


def dot_nt(left, right):
    return lax.dot_general(left, right, (((1,), (1,)), ((), ())), preferred_element_type=F32)


def dot_tn(left, right):
    return lax.dot_general(left, right, (((0,), (0,)), ((), ())), preferred_element_type=F32)


def rows_of(shape, axis):
    return lax.broadcasted_iota(jnp.int32, shape, axis)


MESH = pl.DeviceIdType.MESH
DEVICES = 128
BLOCK = 256
WIDE = 512


class Place:
    def __init__(self):
        self.a, self.b = lax.axis_index("nz"), lax.axis_index("nx")
        self.me = self.a * 32 + self.b
        self.core = self.a & 1
        self.beside = (self.a, self.b ^ 1)
        self.sign = 1 - 2 * self.core
        y = (self.a >> 1) * 2 + ((self.b >> 2) & 1)
        ys = [(y + self.sign * d) & 3 for d in range(4)]
        self.xs = [(self.b + self.sign * d) & 3 for d in range(4)]
        self.ys = [((d >> 1) * 2, (d & 1) * 4) for d in ys]
        self.z = self.b >> 3

    def each(self, visit):
        def some(j, carry):
            core = self.core ^ (j >> 2)
            z = self.z + self.sign * (j & 3)
            for v in range(4):
                for u in range(4):
                    y_hi, y_lo = self.ys[(u + v) & 3]
                    nz = y_hi + core
                    nx = ((z + self.sign * (3 * u + 2 * v)) & 3) * 8 + y_lo + self.xs[u]
                    if u or v:
                        visit(nz, nx)
                    else:
                        pl.when(j > 0)(lambda nz=nz, nx=nx: visit(nz, nx))
            return carry

        lax.fori_loop(0, 8, some, 0)


def transfer(src, dst, sems, device):
    return pltpu.make_async_remote_copy(
        src_ref=src, dst_ref=dst, send_sem=sems.at[0], recv_sem=sems.at[1], device_id=device, device_id_type=MESH
    )


def scatter(place, src, dst, sems, own_sem):
    own = pltpu.make_async_copy(src.at[place.me], dst.at[place.me], own_sem)
    own.start()

    def send(a, b):
        transfer(src.at[a * 32 + b], dst.at[place.me], sems, (a, b)).start()

    place.each(send)
    own.wait()


def all_chunks(place, src, dst, sems):
    others = pl.ds(0, DEVICES - 1)
    return transfer(src.at[others], dst.at[others], sems, place.beside)


def stage_modes(modes_ref, stage_ref, h):
    streams, spans, _ = modes_ref.shape
    half = streams // HALVES
    for k in range(half):
        stage_ref[pl.ds(k * WINDOW, spans), :] = modes_ref[h * half + k].astype(F32)


def synth_y(h, stage_ref, table_ref, work_ref):
    def columns(i, carry):
        lines = dot_nt(table_ref[...], stage_ref[pl.ds(pl.multiple_of(i * BLOCK, BLOCK), BLOCK), :].astype(BF16))
        lane = pl.ds(pl.multiple_of((i & 1) * BLOCK, BLOCK), BLOCK)
        work_ref[2 * h + (i >> 1), 0 : lines.shape[0], lane] = lines
        return carry

    lax.fori_loop(0, LANES // BLOCK, columns, 0)


def pack_chunks(work_ref, chunk_ref):
    rows = DEVICES * PLANES

    def pack(i, carry):
        lane = pl.ds(pl.multiple_of((i & 3) * TILE, TILE), TILE)
        low = work_ref[i >> 2, 0:rows, lane].reshape(rows // 8, 8, TILE)
        high = work_ref[2 + (i >> 2), 0:rows, lane].reshape(rows // 8, 8, TILE)
        upper = rows_of(low.shape, 1) < 4
        even = jnp.where(upper, low, pltpu.roll(high, 4, 1))
        odd = jnp.where(upper, pltpu.roll(low, 4, 1), high)
        both = jnp.stack([even, odd], axis=1).reshape(DEVICES, 8, TILE)
        chunk_ref[:, :, pl.ds(pl.multiple_of(i * TILE, TILE), TILE)] = both.astype(BF16)
        return carry

    lax.fori_loop(0, LANES // TILE, pack, 0)


def unpack_rows(chunk_ref, h, at):
    chunk = chunk_ref[:, :, at].astype(F32)
    width = chunk.shape[2]
    pairs = chunk.reshape(DEVICES // 2, 2, 8, width)
    even, odd = pairs[:, 0], pairs[:, 1]
    upper = rows_of(even.shape, 1) < 4
    if h == 0:
        rows = jnp.where(upper, even, pltpu.roll(odd, 4, 1))
    else:
        rows = jnp.where(upper, pltpu.roll(even, 4, 1), odd)
    return rows.reshape(DEVICES * PLANES, width).astype(BF16)


def window_place(k):
    off = k * WINDOW
    first, shift = off >> 7, off & (TILE - 1)
    at = pl.ds(pl.multiple_of(first * TILE, TILE), TILE)
    after = pl.ds(pl.multiple_of((first + 1) * TILE, TILE), TILE)
    return shift, at, after


def synth_z(chunk_ref, table_ref, plane_ref, stage_ref, planes):
    group = DEVICES // 4
    rows = group * 8
    part = rows // PLANES

    def window(k, carry):
        shift, at, after = window_place(k)
        parts = []
        for a in range(4):
            own = pl.ds(a * group, group)
            left = chunk_ref[own, :, at].astype(F32).reshape(rows, TILE)
            right = chunk_ref[own, :, after].astype(F32).reshape(rows, TILE)
            mixed = jnp.where(rows_of(left.shape, 1) >= shift, left, right)
            parts.append(pltpu.roll(mixed, (TILE - shift) & (TILE - 1), 1).astype(BF16))
        points = dot(jnp.concatenate(parts, axis=1), table_ref[...])
        for c in range(NZ // TILE):
            stage_ref[c] = points[:, c * TILE : (c + 1) * TILE]
            for p in range(planes):
                plane_ref[p, pl.ds(pl.multiple_of(k * part, part), part), c * TILE : (c + 1) * TILE] = stage_ref[
                    c, pl.ds(p, part, stride=PLANES), :
                ].astype(BF16)
        return carry

    lax.fori_loop(0, 11, window, 0)


def analyse_z(stream_ref, table_ref, chunk_ref):
    group = DEVICES // 4

    def window(k, carry):
        shift, at, after = window_place(k)
        points = jnp.concatenate([stream_ref[k, c].astype(BF16) for c in range(NZ // TILE)], axis=1)
        lines = dot(points, table_ref[...])
        for a in range(4):
            own = pl.ds(a * group, group)
            moved = pltpu.roll(lines[:, a * TILE : (a + 1) * TILE], shift, 1).reshape(group, 8, TILE)
            keep = rows_of(moved.shape, 2) >= shift
            chunk_ref[own, :, at] = jnp.where(keep, moved, chunk_ref[own, :, at].astype(F32)).astype(BF16)
            chunk_ref[own, :, after] = moved.astype(BF16)
        return carry

    lax.fori_loop(0, 11, window, 0)


def keep_lines(stream_ref, lines, p, c):
    part = lines.shape[0] // 11
    for k in range(11):
        for t in range(BLOCK // TILE):
            stream_ref[k, c * (BLOCK // TILE) + t, pl.ds(p, part, stride=PLANES), :] = lines[
                k * part : (k + 1) * part, t * TILE : (t + 1) * TILE
            ]


def column_loop(body):
    def step(c, carry):
        body(c, pl.ds(pl.multiple_of(c * BLOCK, BLOCK), BLOCK))
        return carry

    lax.fori_loop(0, NZ // BLOCK, step, 0)


SPARE = 72
LAST = slice(LANES - TILE, LANES)


def last_out(place, work_ref, table_ref, rows_ref):
    lane = rows_of((1, TILE), 1)
    points = DEVICES * PLANES
    table = table_ref[:, pl.ds(pl.multiple_of(place.a * TILE, TILE), TILE)]
    for h in range(HALVES):
        for k in range(11):
            first, shift = divmod(k * WINDOW, TILE)
            tile = lambda t: work_ref[2 * h + t // 4, points : points + 1, (t % 4) * TILE : (t % 4 + 1) * TILE]
            row = tile(first)
            if shift:
                row = pltpu.roll(jnp.where(lane >= shift, row, tile(first + 1)), TILE - shift, 1)
            rows_ref[SPARE + k : SPARE + k + 1, :] = row
        work_ref[2 * h + 1, 0:points, WIDE - TILE : WIDE] += dot_nt(table, rows_ref[...].astype(BF16))


def last_in(chunk_ref, points_ref, last_ref):
    group = DEVICES // 4
    total = chunk_ref[0:group, :, LAST].astype(F32)
    for a in range(1, 4):
        total = total + chunk_ref[a * group : (a + 1) * group, :, LAST].astype(F32)
    points_ref[0] = total.reshape(group * 8, TILE)
    part = group * HALVES
    lines = [points_ref[0, pl.ds(p, part, stride=PLANES), :] for p in range(PLANES)]
    lane = rows_of((part, TILE), 1)
    for k in range(11):
        rows = jnp.zeros((part, TILE), F32)
        for p in range(PLANES):
            rows = jnp.where(lane == p, lines[p][:, SPARE + k : SPARE + k + 1], rows)
        last_ref[k * part : (k + 1) * part, :] = rows.astype(BF16)


def last_back(lines, points_ref):
    part = lines.shape[0] // 11
    lane = rows_of((part, TILE), 1)
    for p in range(PLANES):
        rows = jnp.zeros((part, TILE), F32)
        for k in range(11):
            rows = jnp.where(lane == SPARE + k, lines[k * part : (k + 1) * part, p : p + 1], rows)
        points_ref[1, pl.ds(p, part, stride=PLANES), :] = rows


def last_fill(points_ref, chunk_ref):
    group = DEVICES // 4
    rows = points_ref[1].reshape(group, 8, TILE)
    keep = rows_of(rows.shape, 2) < SPARE
    for a in range(4):
        own = slice(a * group, (a + 1) * group)
        chunk_ref[own, :, LAST] = jnp.where(keep, chunk_ref[own, :, LAST].astype(F32), rows).astype(BF16)


def last_edge(place, chunk_ref, table_ref, edge_ref):
    table = table_ref[:, pl.ds(pl.multiple_of(place.a * TILE, TILE), TILE)]
    lane = rows_of((1, TILE), 1)
    for h in range(HALVES):
        lines = dot_tn(unpack_rows(chunk_ref, h, LAST), table).astype(BF16).astype(F32)
        for k in range(11):
            first, shift = divmod(k * WINDOW, TILE)
            moved = lines[SPARE + k : SPARE + k + 1]
            here, after = slice(first * TILE, (first + 1) * TILE), slice((first + 1) * TILE, (first + 2) * TILE)
            if shift:
                moved = pltpu.roll(moved, shift, 1)
                edge_ref[h, 0:1, here] = jnp.where(lane >= shift, moved, edge_ref[h, 0:1, here])
            else:
                edge_ref[h, 0:1, here] = moved
            edge_ref[h, 0:1, after] = moved


def wave_squares(place, half_span, half_stream, span_local, stream_local, h, start):
    lane = start + rows_of((1, WIDE), 1)
    k, j = lane // WINDOW, lane % WINDOW

    def squared(mode, count):
        wave = 2.0 * jnp.where(mode < count, mode, mode - count + 1).astype(F32) / count
        return wave * wave

    stream = squared(place.b * stream_local + h * (stream_local // HALVES) + k, half_stream)
    return squared(place.a * span_local + j, half_span) + stream


def kernel(
    phi_hbm, vel_hbm, points_hbm, synth_zt_hbm, synth_z_hbm, synth_x_hbm, analy_x_hbm, analy_z_hbm, analy_y_hbm, slope_hbm,
    dual_hbm, basis_hbm, rates_ref, out_ref,
    modes_ref, table_y_ref, synth_zt_ref, synth_z_ref, synth_x_ref, analy_x_ref, analy_z_ref, analy_y_ref, slope_ref,
    dual_ref, basis_ref, stage_ref, work_ref, solve_ref, plane_ref, points_ref, stream_ref, rows_ref, last_ref, last_phi_ref,
    edge_ref, eig_ref, cube_table, flux_table, both_table, ends_ref,
    phi_send, vel_send, phi_recv, vel_recv, cube_recv, flux_recv,
    table_sems, modes_sem, own_sem, phi_sems, vel_sems, cube_sems, flux_sems,
):
    place = Place()
    cheb = dual_ref.shape[0]
    streams, spans, _ = modes_ref.shape
    rows = cheb - 1

    modes_copy = pltpu.make_async_copy(phi_hbm, modes_ref, modes_sem)
    modes_copy.start()
    moves = {}
    pairs = dict(
        points=(points_hbm, table_y_ref), synth_zt=(synth_zt_hbm, synth_zt_ref), dual=(dual_hbm, dual_ref),
        analy_y=(analy_y_hbm, analy_y_ref), slope=(slope_hbm, slope_ref), basis=(basis_hbm, basis_ref),
        synth_z=(synth_z_hbm, synth_z_ref), synth_x=(synth_x_hbm, synth_x_ref), analy_x=(analy_x_hbm, analy_x_ref),
        analy_z=(analy_z_hbm, analy_z_ref),
    )
    for i, (name, (src, dst)) in enumerate(pairs.items()):
        moves[name] = pltpu.make_async_copy(src, dst, table_sems.at[i])
        moves[name].start()

    barrier = pltpu.get_barrier_semaphore()

    def greet(a, b):
        pl.semaphore_signal(barrier, inc=1, device_id=(a, b), device_id_type=MESH)

    place.each(greet)

    stage_ref[...] = jnp.zeros_like(stage_ref)
    rows_ref[...] = jnp.zeros_like(rows_ref)
    modes_copy.wait()
    stage_modes(modes_ref, stage_ref, 0)
    moves["points"].wait()
    synth_y(0, stage_ref, table_y_ref, work_ref)
    stage_modes(modes_ref, stage_ref, 1)
    synth_y(1, stage_ref, table_y_ref, work_ref)
    moves["synth_zt"].wait()
    last_out(place, work_ref, synth_zt_ref, rows_ref)
    pack_chunks(work_ref, phi_send)
    pl.semaphore_wait(barrier, DEVICES - 1)
    scatter(place, phi_send, phi_recv, phi_sems, own_sem)

    moves["dual"].wait()
    for h in (1, 0):
        if h == 0:
            stage_modes(modes_ref, stage_ref, 0)
            vel_copy = pltpu.make_async_copy(vel_hbm, modes_ref, modes_sem)
            vel_copy.start()

        def dual_columns(i, carry, h=h):
            at = pl.ds(pl.multiple_of(i * BLOCK, BLOCK), BLOCK)
            solve_ref[h, :, at] = dot_nt(dual_ref[...], stage_ref[at, :].astype(BF16))
            return carry

        lax.fori_loop(0, LANES // BLOCK, dual_columns, 0)

    vel_copy.wait()
    for h in range(HALVES):
        stage_modes(modes_ref, stage_ref, h)
        synth_y(h, stage_ref, table_y_ref, work_ref)
    last_out(place, work_ref, synth_zt_ref, rows_ref)
    pack_chunks(work_ref, vel_send)
    scatter(place, vel_send, vel_recv, vel_sems, own_sem)

    for name in ("analy_y", "slope", "basis"):
        moves[name].wait()
    for n, (left, product) in enumerate(((analy_y_ref, cube_table), (slope_ref, flux_table))):
        full = dot(dual_ref[...], left[...])
        product[...] = full[:, 0:rows].astype(BF16)
        ends_ref[n] = jnp.broadcast_to(full[:, rows:cheb], (cheb, TILE))
    both_table[...] = dot(dual_ref[...], basis_ref[...]).astype(BF16)
    eig_ref[0:rows, :] = -jnp.transpose(jnp.broadcast_to(rates_ref[:, 0:rows], (TILE, rows)))
    eig_ref[rows:cheb, :] = -jnp.broadcast_to(rates_ref[:, rows:cheb], (1, TILE))

    for name in ("synth_z", "synth_x", "analy_x", "analy_z"):
        moves[name].wait()
    all_chunks(place, phi_send, phi_recv, phi_sems).wait_recv()
    synth_z(phi_recv, synth_z_ref, plane_ref, points_ref, PLANES)
    for p in range(PLANES):

        def cube_columns(c, at, p=p):
            phi = dot(synth_x_ref[...], plane_ref[p, :, at])
            work_ref[p, :, at] = phi
            keep_lines(stream_ref, dot(analy_x_ref[...], (phi * phi * phi).astype(BF16)), p, c)

        column_loop(cube_columns)

    last_in(phi_recv, points_ref, last_ref)
    phi = dot(synth_x_ref[...], last_ref[...])
    last_phi_ref[...] = phi
    last_back(dot(analy_x_ref[...], (phi * phi * phi).astype(BF16)), points_ref)
    all_chunks(place, phi_send, phi_recv, phi_sems).wait_send()
    analyse_z(stream_ref, analy_z_ref, phi_send)
    last_fill(points_ref, phi_send)
    scatter(place, phi_send, cube_recv, cube_sems, own_sem)

    all_chunks(place, vel_send, vel_recv, vel_sems).wait_recv()
    synth_z(vel_recv, synth_z_ref, plane_ref, points_ref, PLANES)
    for p in range(PLANES):

        def flux_columns(c, at, p=p):
            flux = dot(synth_x_ref[...], plane_ref[p, :, at]) * work_ref[p, :, at]
            keep_lines(stream_ref, dot(analy_x_ref[...], flux.astype(BF16)), p, c)

        column_loop(flux_columns)

    last_in(vel_recv, points_ref, last_ref)
    flux = dot(synth_x_ref[...], last_ref[...]) * last_phi_ref[...]
    last_back(dot(analy_x_ref[...], flux.astype(BF16)), points_ref)
    all_chunks(place, vel_send, vel_recv, vel_sems).wait_send()
    analyse_z(stream_ref, analy_z_ref, vel_send)
    last_fill(points_ref, vel_send)
    scatter(place, vel_send, flux_recv, flux_sems, own_sem)

    def squares_at(h, start):
        return wave_squares(place, spans * 2, streams * 16, spans, streams, h, start)

    eig = eig_ref[:, 0:1]
    all_chunks(place, phi_send, cube_recv, cube_sems).wait_recv()
    last_edge(place, cube_recv, analy_z_ref, edge_ref)
    for h in range(HALVES):

        def lap_columns(i, carry, h=h):
            at = pl.ds(pl.multiple_of(i * WIDE, WIDE), WIDE)
            phi = solve_ref[h, :, at]
            cube = dot(cube_table[...], unpack_rows(cube_recv, h, at)) + ends_ref[0, :, 0:1] * edge_ref[h, 0:1, at]
            scaled = (eig - squares_at(h, i * WIDE)) * (cube - (1.0 + stabilizer) * phi)
            lap = dot(both_table[...], scaled.astype(BF16))
            solve_ref[h, :, at] = (phi / time_step + mobility * lap) / (capillary * mobility)
            return carry

        lax.fori_loop(0, LANES // WIDE, lap_columns, 0)
    all_chunks(place, vel_send, flux_recv, flux_sems).wait_recv()
    last_edge(place, flux_recv, analy_z_ref, edge_ref)
    for h in range(HALVES):

        def solve_columns(i, carry, h=h):
            at = pl.ds(pl.multiple_of(i * WIDE, WIDE), WIDE)
            shifted = eig - squares_at(h, i * WIDE)
            slope = dot(flux_table[...], unpack_rows(flux_recv, h, at)) + ends_ref[1, :, 0:1] * edge_ref[h, 0:1, at]
            forcing = solve_ref[h, :, at] - 8.0 / (cheb - 1) / (capillary * mobility) * slope
            first = (forcing / (shifted - screen_low)).astype(BF16)
            out_ref[h, :, at] = (dot(both_table[...], first) / (shifted - screen_high)).astype(BF16)
            return carry

        lax.fori_loop(0, LANES // WIDE, solve_columns, 0)
    all_chunks(place, phi_send, cube_recv, cube_sems).wait_send()
    all_chunks(place, vel_send, flux_recv, flux_sems).wait_send()


def finish_kernel(second_ref, basis_ref, out_ref):
    half, spans, _ = out_ref.shape
    for start in range(0, LANES, BLOCK):
        result = lax.dot_general(
            second_ref[0, :, start : start + BLOCK], basis_ref[...], (((0,), (1,)), ((), ())), preferred_element_type=F32
        )
        for k in range(half):
            low, high = max(k * WINDOW, start), min(k * WINDOW + spans, start + BLOCK)
            if low < high:
                out_ref[k, low - k * WINDOW : high - k * WINDOW, :] = result[low - start : high - start]


def per_device(phi_hat, vel_hat, helm_basis, helm_dual, helm_rates):
    span_count = lax.axis_size("nz")
    stream_count = lax.axis_size("nx")
    span_local, stream_local, cheb = phi_hat.shape
    half = stream_local // HALVES
    s_x, a_x = fourier_tables(stream_local * stream_count, NX)
    s_z, a_z = fourier_tables(span_local * span_count, NZ)
    s_y, a_y, d_y = chebyshev_tables(cheb)

    points = np.pad(s_y.T, ((0, -cheb % 8), (0, 0)))
    slope = (d_y.astype(np.float64).T @ a_y.astype(np.float64).T).astype(np.float32).astype(BF)
    order = np.arange(stream_local * stream_count).reshape(stream_count, HALVES, half).transpose(2, 0, 1).reshape(-1)
    synth_x = np.ascontiguousarray(s_x.T[:, order])
    analy_x = np.ascontiguousarray(a_x.T[order])
    synth_z = np.pad(s_z.reshape(span_count, span_local, NZ), ((0, 0), (0, TILE - span_local), (0, 0))).reshape(-1, NZ)
    analy_z = np.pad(a_z.reshape(NZ, span_count, span_local), ((0, 0), (0, 0), (0, TILE - span_local))).reshape(NZ, -1)

    large = [jnp.transpose(phi_hat, (1, 0, 2)), jnp.transpose(vel_hat, (1, 0, 2))]
    tables = (points, np.ascontiguousarray(synth_z.T), synth_z, synth_x, analy_x, analy_z, np.ascontiguousarray(a_y.T), slope)
    large += [jnp.asarray(table) for table in tables] + [helm_dual, helm_basis]
    modes_x = stream_local * stream_count
    chunk = pltpu.VMEM((DEVICES, 8, LANES), BF16)
    sems = pltpu.SemaphoreType.DMA((2,))
    second = pl.pallas_call(
        kernel,
        out_shape=jax.ShapeDtypeStruct((HALVES, cheb, LANES), BF16),
        in_specs=[pl.BlockSpec(memory_space=pl.ANY)] * len(large) + [pl.BlockSpec(memory_space=pltpu.VMEM)],
        out_specs=pl.BlockSpec(memory_space=pltpu.VMEM),
        scratch_shapes=[pltpu.VMEM(large[0].shape, BF16)]
        + [pltpu.VMEM(table.shape, BF16) for table in large[2:]]
        + [
            pltpu.VMEM((LANES, cheb), F32),
            pltpu.VMEM((PLANES, NX, NZ), F32),
            pltpu.VMEM((HALVES, cheb, LANES), F32),
            pltpu.VMEM((PLANES, modes_x, NZ), BF16),
            pltpu.VMEM((NZ // TILE, 256, TILE), F32),
            pltpu.VMEM((11, NZ // TILE, 256, TILE), F32),
            pltpu.VMEM((TILE, TILE), F32),
            pltpu.VMEM((modes_x, TILE), BF16),
            pltpu.VMEM((NX, TILE), F32),
            pltpu.VMEM((HALVES, 8, LANES), F32),
            pltpu.VMEM((cheb, TILE), F32),
            pltpu.VMEM((cheb, cheb - 1), BF16),
            pltpu.VMEM((cheb, cheb - 1), BF16),
            pltpu.VMEM((cheb, cheb), BF16),
            pltpu.VMEM((2, cheb, TILE), F32),
        ]
        + [chunk] * 6
        + [
            pltpu.SemaphoreType.DMA((len(large) - 2,)), pltpu.SemaphoreType.DMA, pltpu.SemaphoreType.DMA,
            sems, sems, sems, sems,
        ],
        compiler_params=pltpu.CompilerParams(collective_id=0, has_side_effects=True, vmem_limit_bytes=60 << 20),
    )(*large, helm_rates.reshape(1, cheb))
    result = pl.pallas_call(
        finish_kernel,
        out_shape=jax.ShapeDtypeStruct((stream_local, span_local, cheb), F32),
        grid=(HALVES,),
        in_specs=[pl.BlockSpec((1, cheb, LANES), lambda h: (h, 0, 0)), pl.BlockSpec((cheb, cheb), lambda h: (0, 0))],
        out_specs=pl.BlockSpec((half, span_local, cheb), lambda h: (h, 0, 0)),
        compiler_params=pltpu.CompilerParams(vmem_limit_bytes=40 << 20),
    )(second, helm_basis)
    return jnp.transpose(result, (1, 0, 2))


def solution(mesh):
    placed = (P("nz", "nx", None), P("nz", "nx", None), P(), P(), P())
    return jax.shard_map(
        per_device, mesh=mesh, in_specs=placed, out_specs=P("nz", "nx", None), check_vma=False
    )
```

time: 182 us -> 134 us (0.74)
  Pallas kernels: 169 us -> 131 us
  local copies, waits for them, and re-layouts: 10.9 us -> 2.86 us
    pallas_call x1 -> x2, Pallas kernels: 169 us -> 131 us  [the longest x1 127 us: per_device(): pl.pallas_call(kernel, out_shape=jax.ShapeDtypeStruct((HALVES, cheb, LANE...]
    unnamed x2 -> x4, local copies, waits for them, and re-layouts: 7.19 us -> 1.6 us
where the time goes in v2:
time: 134 us
  Pallas kernels  131 us (98%)
  local copies, waits for them, and re-layouts  2.86 us (2%)
    pallas_call x1, Pallas kernels, per_device(): pl.pallas_call(kernel, out_shape=jax.ShapeDtypeStruct((HALVES, cheb, LANE...  127 us
    pallas_call x1, Pallas kernels, per_device(): pl.pallas_call(finish_kernel, out_shape=jax.ShapeDtypeStruct((stream_loca...  4.31 us

profile of v2, /device:TPU:1, one launch (start us, length us, event | category | flops | bytes accessed | tf_op | source)
XLA Modules:
  0.0 133.9 jit_solution(12165831144549240006)
XLA Ops:
  0.0 1.3 reshape.3.rates_ref
  1.3 0.0 copy-start.1
  1.3 126.7 %shard_map.127.second_ref = bf16[2,513,1024]{2,1,0:T(8,128)(2,1)} custom-call(bf16[22,86,513]{2,1,0:T(8,128)(2,1)} %bitcast.3, bf16[22,86,513]{2,1,0:T(8,128)(2,1)} %bitcast.4, bf16[520,513]{1,0:T(8,128)(2,1)} %constant.16.clone.points_hbm, bf16[512,512]{1,0:T(8,128)(2,1)} %constant.17.clone.synth_zt_hbm, bf16[512,512]{1,0:T(8,128)(2,1)} %constant.18.clone.synth_z_hbm, ...), custom_call_target="tpu_custom_call" | custom-call | tf_op jit(solution)/shard_map/pallas_call | solution.py:525
  127.9 0.0 copy-done.1
  127.9 0.0 copy-start
  127.9 1.6 %copy-done = bf16[2,513,1024]{2,1,0:T(8,128)(2,1)S(1)} copy-done((bf16[2,513,1024]{2,1,0:T(8,128)(2,1)S(1)}, bf16[2,513,1024]{2,1,0:T(8,128)(2,1)}, u32[]{:S(2)}) %copy-start) | copy-done | bytes 2101272
  129.5 4.3 %shard_map.128 = f32[22,86,513]{2,1,0:T(8,128)} custom-call(bf16[2,513,1024]{2,1,0:T(8,128)(2,1)S(1)} %copy-done, bf16[513,513]{1,0:T(8,128)(2,1)S(1)} %copy-done.1), custom_call_target="tpu_custom_call" | custom-call | tf_op jit(solution)/shard_map/pallas_call | solution.py:556
Async XLA Ops:
  1.3 126.7 %copy-start.1 = (bf16[513,513]{1,0:T(8,128)(2,1)S(1)}, bf16[513,513]{1,0:T(8,128)(2,1)}, u32[]{:S(2)}) copy-start(bf16[513,513]{1,0:T(8,128)(2,1)} %basis_ref.1) | copy-start | bytes 1579018
  127.9 1.6 %copy-start = (bf16[2,513,1024]{2,1,0:T(8,128)(2,1)S(1)}, bf16[2,513,1024]{2,1,0:T(8,128)(2,1)}, u32[]{:S(2)}) copy-start(bf16[2,513,1024]{2,1,0:T(8,128)(2,1)} %shard_map.127.second_ref) | copy-start | bytes 6303748

commit v3 on v2

v3 whole, which is shorter than its diff:
```python
import math

import jax
import jax.numpy as jnp
import ml_dtypes
import numpy as np
from jax import lax
from jax.experimental import pallas as pl
from jax.experimental.pallas import tpu as pltpu
from jax.sharding import PartitionSpec as P

NX = 1024
NZ = 512

mobility = 1.0
capillary = 0.2
screen_low = 4.0
screen_high = 20.0
time_step = 1.0 / (screen_low * screen_high * mobility * capillary)
stabilizer = capillary * (screen_low + screen_high)

PLANES = 4
HALVES = 2
WINDOW = 88
LANES = 1024
TILE = 128
BF = ml_dtypes.bfloat16
F32 = jnp.float32
BF16 = jnp.bfloat16


def fourier_tables(mode_count, point_count):
    half_count = mode_count // 2
    mode_index = np.arange(mode_count)
    wave_index = np.where(mode_index < half_count, mode_index, mode_index - half_count + 1)
    phase_steps = wave_index[:, None] * np.arange(point_count)[None, :] % point_count
    angles = phase_steps * (2.0 * math.pi / point_count)
    basis = np.where((mode_index < half_count)[:, None], np.cos(angles), np.sin(angles))
    factor = math.sqrt(2.0 / mode_count)
    weights = np.where(mode_index == 0, 1.0, 2.0) / (point_count * factor)
    return (
        (factor * basis).astype(np.float32).astype(BF),
        (basis.T * weights[None, :]).astype(np.float32).astype(BF),
    )


def chebyshev_tables(count):
    index = np.arange(count)
    phase_steps = index[:, None] * index[None, :] % (2 * (count - 1))
    cosines = np.cos(phase_steps * (math.pi / (count - 1)))
    factor = math.sqrt(2.0 / count)
    ends = np.where((index == 0) | (index == count - 1), 2.0, 1.0)
    analysis = cosines.T * (2.0 / ((count - 1) * factor)) / (ends[:, None] * ends[None, :])
    upper, lower = index[:, None], index[None, :]
    deriv = np.where((upper > lower) & ((upper + lower) % 2 == 1), 2.0 * upper / ends[None, :], 0.0)
    as_bf = lambda t: t.astype(np.float32).astype(BF)
    return as_bf(factor * cosines), as_bf(analysis), as_bf(deriv)


def dot(left, right):
    return jnp.dot(left, right, preferred_element_type=F32)


def dot_nt(left, right):
    return lax.dot_general(left, right, (((1,), (1,)), ((), ())), preferred_element_type=F32)


def dot_tn(left, right):
    return lax.dot_general(left, right, (((0,), (0,)), ((), ())), preferred_element_type=F32)


def rows_of(shape, axis):
    return lax.broadcasted_iota(jnp.int32, shape, axis)


MESH = pl.DeviceIdType.MESH
DEVICES = 128
BLOCK = 256
WIDE = 512
BASE = LANES - 11 * WINDOW


class Place:
    def __init__(self):
        self.a, self.b = lax.axis_index("nz"), lax.axis_index("nx")
        self.me = self.a * 32 + self.b
        self.core = self.a & 1
        self.beside = (self.a, self.b ^ 1)
        self.sign = 1 - 2 * self.core
        y = (self.a >> 1) * 2 + ((self.b >> 2) & 1)
        ys = [(y + self.sign * d) & 3 for d in range(4)]
        self.xs = [(self.b + self.sign * d) & 3 for d in range(4)]
        self.ys = [((d >> 1) * 2, (d & 1) * 4) for d in ys]
        self.z = self.b >> 3

    def each(self, visit):
        def some(j, carry):
            core = self.core ^ (j >> 2)
            z = self.z + self.sign * (j & 3)
            for v in range(4):
                for u in range(4):
                    y_hi, y_lo = self.ys[(u + v) & 3]
                    nz = y_hi + core
                    nx = ((z + self.sign * (3 * u + 2 * v)) & 3) * 8 + y_lo + self.xs[u]
                    if u or v:
                        visit(nz, nx)
                    else:
                        pl.when(j > 0)(lambda nz=nz, nx=nx: visit(nz, nx))
            return carry

        lax.fori_loop(0, 8, some, 0)


def transfer(src, dst, sems, device):
    return pltpu.make_async_remote_copy(
        src_ref=src, dst_ref=dst, send_sem=sems.at[0], recv_sem=sems.at[1], device_id=device, device_id_type=MESH
    )


def lanes_of(g):
    return slice(g * WIDE, (g + 1) * WIDE)


def scatter(place, src, dst, sems, own_sem, g):
    own = pltpu.make_async_copy(src.at[place.me, :, lanes_of(g)], dst.at[place.me, :, lanes_of(g)], own_sem)
    own.start()

    def send(a, b):
        transfer(src.at[a * 32 + b, :, lanes_of(g)], dst.at[place.me, :, lanes_of(g)], sems.at[g], (a, b)).start()

    place.each(send)
    own.wait()


def all_chunks(place, src, dst, sems, g):
    others = pl.ds(0, DEVICES - 1)
    return transfer(src.at[others, :, lanes_of(g)], dst.at[others, :, lanes_of(g)], sems.at[g], place.beside)


def stage_modes(modes_ref, stage_ref, g, base):
    streams, spans, _ = modes_ref.shape
    half = streams // HALVES
    for h in range(HALVES):
        for k in range(half):
            off = base + k * WINDOW
            low, high = max(off, g * WIDE), min(off + spans, (g + 1) * WIDE)
            if low < high:
                rows = modes_ref[h * half + k].astype(F32)[low - off : high - off]
                stage_ref[(h - g) * WIDE + low : (h - g) * WIDE + high, :] = rows


def synth_y(g, stage_ref, table_ref, work_ref):
    def columns(h, carry):
        lines = dot_nt(table_ref[...], stage_ref[pl.ds(pl.multiple_of(h * WIDE, WIDE), WIDE), :].astype(BF16))
        work_ref[2 * h + g, 0 : lines.shape[0], :] = lines
        return carry

    lax.fori_loop(0, HALVES, columns, 0)


def pack_chunks(work_ref, chunk_ref, g):
    rows = DEVICES * PLANES

    def pack(i, carry):
        lane = pl.ds(pl.multiple_of(i * TILE, TILE), TILE)
        low = work_ref[g, 0:rows, lane].reshape(rows // 8, 8, TILE)
        high = work_ref[2 + g, 0:rows, lane].reshape(rows // 8, 8, TILE)
        upper = rows_of(low.shape, 1) < 4
        even = jnp.where(upper, low, pltpu.roll(high, 4, 1))
        odd = jnp.where(upper, pltpu.roll(low, 4, 1), high)
        both = jnp.stack([even, odd], axis=1).reshape(DEVICES, 8, TILE)
        chunk_ref[:, :, pl.ds(pl.multiple_of(g * WIDE + i * TILE, TILE), TILE)] = both.astype(BF16)
        return carry

    lax.fori_loop(0, WIDE // TILE, pack, 0)


def unpack_rows(chunk_ref, h, at):
    chunk = chunk_ref[:, :, at].astype(F32)
    width = chunk.shape[2]
    pairs = chunk.reshape(DEVICES // 2, 2, 8, width)
    even, odd = pairs[:, 0], pairs[:, 1]
    upper = rows_of(even.shape, 1) < 4
    if h == 0:
        rows = jnp.where(upper, even, pltpu.roll(odd, 4, 1))
    else:
        rows = jnp.where(upper, pltpu.roll(even, 4, 1), odd)
    return rows.reshape(DEVICES * PLANES, width).astype(BF16)


def tile_of(t):
    return slice(t * TILE, (t + 1) * TILE)


def fill_windows(chunk_ref, lines_ref, ks):
    group = DEVICES // 4
    rows = group * 8
    for k in ks:
        first, shift = divmod(k * WINDOW, TILE)
        for a in range(4):
            own = slice(a * group, (a + 1) * group)
            part = chunk_ref[own, :, tile_of(first)].astype(F32).reshape(rows, TILE)
            if shift + WINDOW > TILE:
                right = chunk_ref[own, :, tile_of(first + 1)].astype(F32).reshape(rows, TILE)
                part = jnp.where(rows_of(part.shape, 1) >= shift, part, right)
            if shift:
                part = pltpu.roll(part, TILE - shift, 1)
            lines_ref[k * rows : (k + 1) * rows, tile_of(a)] = part.astype(BF16)


def synth_z(lines_ref, table_ref, plane_ref, stage_ref, ks):
    low, high = ks[0] * 256, (ks[-1] + 1) * 256
    part = (high - low) // PLANES
    for c in range(NZ // BLOCK):
        points = dot(lines_ref[low:high, :], table_ref[:, c * BLOCK : (c + 1) * BLOCK])
        for t in range(BLOCK // TILE):
            stage_ref[t, 0 : high - low, :] = points[:, tile_of(t)]
            for p in range(PLANES):
                plane_ref[p, low // PLANES : high // PLANES, tile_of(c * (BLOCK // TILE) + t)] = stage_ref[
                    t, pl.ds(p, part, stride=PLANES), :
                ].astype(BF16)


def analyse_z(stream_ref, lines_ref, table_ref, chunk_ref, ks):
    group = DEVICES // 4
    rows = group * 8
    low, high = ks[0] * rows, (ks[-1] + 1) * rows
    for c in range(NZ // TILE):
        lines_ref[low:high, tile_of(c)] = stream_ref[c, low:high, :].astype(BF16)
    for pair in range(2):
        lines = dot(lines_ref[low:high, :], table_ref[:, pair * 2 * TILE : (pair + 1) * 2 * TILE])
        for k in ks:
            first, shift = divmod(BASE + k * WINDOW, TILE)
            for n in range(2):
                own = slice((2 * pair + n) * group, (2 * pair + n + 1) * group)
                moved = lines[k * rows - low : (k + 1) * rows - low, tile_of(n)]
                if not shift:
                    chunk_ref[own, :, tile_of(first)] = moved.reshape(group, 8, TILE).astype(BF16)
                    continue
                moved = pltpu.roll(moved, shift, 1).reshape(group, 8, TILE)
                keep = rows_of(moved.shape, 2) >= shift
                chunk_ref[own, :, tile_of(first)] = jnp.where(
                    keep, moved, chunk_ref[own, :, tile_of(first)].astype(F32)
                ).astype(BF16)
                if shift + WINDOW > TILE:
                    chunk_ref[own, :, tile_of(first + 1)] = moved.astype(BF16)


def keep_lines(stream_ref, lines, p):
    for t in range(NZ // TILE):
        stream_ref[t, pl.ds(p, lines.shape[0], stride=PLANES), :] = lines[:, tile_of(t)]


SPARE = 72
LAST = slice(LANES - TILE, LANES)


def last_out(place, work_ref, table_ref, rows_ref):
    lane = rows_of((1, TILE), 1)
    points = DEVICES * PLANES
    table = table_ref[:, pl.ds(pl.multiple_of(place.a * TILE, TILE), TILE)]
    for h in range(HALVES):
        for k in range(11):
            first, shift = divmod(k * WINDOW, TILE)
            tile = lambda t: work_ref[2 * h + t // 4, points : points + 1, (t % 4) * TILE : (t % 4 + 1) * TILE]
            row = tile(first)
            if shift:
                row = pltpu.roll(jnp.where(lane >= shift, row, tile(first + 1)), TILE - shift, 1)
            rows_ref[SPARE + k : SPARE + k + 1, :] = row
        here = slice(WIDE - TILE, WIDE)
        added = dot_nt(table, rows_ref[...].astype(BF16))
        work_ref[2 * h + 1, 0:points, here] = jnp.where(lane < SPARE, work_ref[2 * h + 1, 0:points, here], added)


def last_in(chunk_ref, points_ref, last_ref):
    group = DEVICES // 4
    total = chunk_ref[0:group, :, LAST].astype(F32)
    for a in range(1, 4):
        total = total + chunk_ref[a * group : (a + 1) * group, :, LAST].astype(F32)
    points_ref[0, 0 : group * 8, :] = total.reshape(group * 8, TILE)
    part = group * HALVES
    lines = [points_ref[0, pl.ds(p, part, stride=PLANES), :] for p in range(PLANES)]
    lane = rows_of((part, TILE), 1)
    for k in range(11):
        rows = jnp.zeros((part, TILE), F32)
        for p in range(PLANES):
            rows = jnp.where(lane == p, lines[p][:, SPARE + k : SPARE + k + 1], rows)
        last_ref[k * part : (k + 1) * part, :] = rows.astype(BF16)


def last_back(lines, points_ref):
    part = lines.shape[0] // 11
    lane = rows_of((part, TILE), 1)
    for p in range(PLANES):
        rows = jnp.zeros((part, TILE), F32)
        for k in range(11):
            rows = jnp.where(lane == k, lines[k * part : (k + 1) * part, p : p + 1], rows)
        points_ref[1, pl.ds(p, part, stride=PLANES), :] = rows


def last_fill(points_ref, chunk_ref):
    group = DEVICES // 4
    rows = points_ref[1, 0 : group * 8, :].reshape(group, 8, TILE)
    keep = rows_of(rows.shape, 2) >= BASE
    for a in range(4):
        own = slice(a * group, (a + 1) * group)
        chunk_ref[own, :, 0:TILE] = jnp.where(keep, chunk_ref[own, :, 0:TILE].astype(F32), rows).astype(BF16)


def last_edge(place, chunk_ref, table_ref, edge_ref):
    table = table_ref[:, pl.ds(pl.multiple_of(place.a * TILE, TILE), TILE)]
    lane = rows_of((1, TILE), 1)
    for h in range(HALVES):
        lines = dot_tn(unpack_rows(chunk_ref, h, slice(0, TILE)), table).astype(BF16).astype(F32)
        for k in range(11):
            first, shift = divmod(BASE + k * WINDOW, TILE)
            moved = lines[k : k + 1]
            if not shift:
                edge_ref[h, 0:1, tile_of(first)] = moved
                continue
            moved = pltpu.roll(moved, shift, 1)
            edge_ref[h, 0:1, tile_of(first)] = jnp.where(lane >= shift, moved, edge_ref[h, 0:1, tile_of(first)])
            if shift + WINDOW > TILE:
                edge_ref[h, 0:1, tile_of(first + 1)] = moved


def wave_squares(place, half_span, half_stream, span_local, stream_local, h, start):
    lane = start - BASE + rows_of((1, WIDE), 1)
    k, j = lane // WINDOW, lane % WINDOW

    def squared(mode, count):
        wave = 2.0 * jnp.where(mode < count, mode, mode - count + 1).astype(F32) / count
        return wave * wave

    stream = squared(place.b * stream_local + h * (stream_local // HALVES) + k, half_stream)
    return squared(place.a * span_local + j, half_span) + stream


def kernel(
    phi_hbm, vel_hbm, points_hbm, synth_zt_hbm, synth_z_hbm, synth_x_hbm, analy_x_hbm, analy_z_hbm, analy_y_hbm, slope_hbm,
    dual_hbm, basis_hbm, rates_ref, out_ref,
    modes_ref, table_y_ref, synth_zt_ref, synth_z_ref, synth_x_ref, analy_x_ref, analy_z_ref, analy_y_ref, slope_ref,
    dual_ref, basis_ref, stage_ref, work_ref, solve_ref, plane_ref, points_ref, lines_ref, stream_ref, rows_ref, last_ref, last_phi_ref,
    edge_ref, eig_ref, both_table, ends_ref,
    phi_send, vel_send, phi_recv, vel_recv, cube_recv, flux_recv,
    table_sems, modes_sem, own_sem, phi_sems, vel_sems, cube_sems, flux_sems,
):
    place = Place()
    cheb = dual_ref.shape[0]
    streams, spans, _ = modes_ref.shape
    rows = cheb - 1

    modes_copy = pltpu.make_async_copy(phi_hbm, modes_ref, modes_sem)
    modes_copy.start()
    moves = {}
    pairs = dict(
        points=(points_hbm, table_y_ref), synth_zt=(synth_zt_hbm, synth_zt_ref), dual=(dual_hbm, dual_ref),
        analy_y=(analy_y_hbm, analy_y_ref), slope=(slope_hbm, slope_ref), basis=(basis_hbm, basis_ref),
        synth_z=(synth_z_hbm, synth_z_ref), synth_x=(synth_x_hbm, synth_x_ref), analy_x=(analy_x_hbm, analy_x_ref),
        analy_z=(analy_z_hbm, analy_z_ref),
    )
    for i, (name, (src, dst)) in enumerate(pairs.items()):
        moves[name] = pltpu.make_async_copy(src, dst, table_sems.at[i])
        moves[name].start()

    barrier = pltpu.get_barrier_semaphore()

    def greet(a, b):
        pl.semaphore_signal(barrier, inc=1, device_id=(a, b), device_id_type=MESH)

    place.each(greet)

    stage_ref[...] = jnp.zeros_like(stage_ref)
    rows_ref[...] = jnp.zeros_like(rows_ref)
    edge_ref[...] = jnp.zeros_like(edge_ref)
    modes_copy.wait()
    stage_modes(modes_ref, stage_ref, 0, 0)
    moves["points"].wait()
    synth_y(0, stage_ref, table_y_ref, work_ref)
    pack_chunks(work_ref, phi_send, 0)
    pl.semaphore_wait(barrier, DEVICES - 1)
    scatter(place, phi_send, phi_recv, phi_sems, own_sem, 0)
    stage_modes(modes_ref, stage_ref, 1, 0)
    synth_y(1, stage_ref, table_y_ref, work_ref)
    moves["synth_zt"].wait()
    last_out(place, work_ref, synth_zt_ref, rows_ref)
    pack_chunks(work_ref, phi_send, 1)
    scatter(place, phi_send, phi_recv, phi_sems, own_sem, 1)

    moves["dual"].wait()
    for g in range(2):
        stage_modes(modes_ref, stage_ref, g, BASE)
        if g == 1:
            vel_copy = pltpu.make_async_copy(vel_hbm, modes_ref, modes_sem)
            vel_copy.start()
        for h in range(HALVES):
            solve_ref[h, :, lanes_of(g)] = dot_nt(dual_ref[...], stage_ref[h * WIDE : (h + 1) * WIDE, :].astype(BF16))

    vel_copy.wait()
    for g in range(2):
        stage_modes(modes_ref, stage_ref, g, 0)
        synth_y(g, stage_ref, table_y_ref, work_ref)
        if g == 1:
            last_out(place, work_ref, synth_zt_ref, rows_ref)
        pack_chunks(work_ref, vel_send, g)
        scatter(place, vel_send, vel_recv, vel_sems, own_sem, g)

    for name in ("analy_y", "slope", "basis"):
        moves[name].wait()
    for n, table in enumerate((analy_y_ref, slope_ref)):
        full = dot(dual_ref[...], table[...])
        table[...] = full.astype(BF16)
        ends_ref[n] = jnp.broadcast_to(full[:, rows:cheb], (cheb, TILE))
    full = dot(dual_ref[...], basis_ref[...])
    both_table[...] = full[:, 0:rows].astype(BF16)
    ends_ref[2] = jnp.broadcast_to(full[:, rows:cheb], (cheb, TILE))
    eig_ref[0:rows, :] = -jnp.transpose(jnp.broadcast_to(rates_ref[:, 0:rows], (TILE, rows)))
    eig_ref[rows:cheb, :] = -jnp.broadcast_to(rates_ref[:, rows:cheb], (1, TILE))

    for name in ("synth_z", "synth_x", "analy_x", "analy_z"):
        moves[name].wait()
    early, late = range(0, 5), range(5, 11)

    def planes_of(send, recv, sems):
        all_chunks(place, send, recv, sems, 0).wait_recv()
        fill_windows(recv, lines_ref, early)
        synth_z(lines_ref, synth_z_ref, plane_ref, points_ref, early)
        all_chunks(place, send, recv, sems, 1).wait_recv()
        fill_windows(recv, lines_ref, late)
        synth_z(lines_ref, synth_z_ref, plane_ref, points_ref, late)
        last_in(recv, points_ref, last_ref)

    def back(send, recv, sems, to, to_sems):
        all_chunks(place, send, recv, sems, 0).wait_send()
        all_chunks(place, send, recv, sems, 1).wait_send()
        analyse_z(stream_ref, lines_ref, analy_z_ref, send, range(0, 6))
        last_fill(points_ref, send)
        scatter(place, send, to, to_sems, own_sem, 0)
        analyse_z(stream_ref, lines_ref, analy_z_ref, send, range(6, 11))
        scatter(place, send, to, to_sems, own_sem, 1)

    planes_of(phi_send, phi_recv, phi_sems)

    def cube_plane(p, carry):
        phi = dot(synth_x_ref[...], plane_ref[p])
        work_ref[p] = phi
        keep_lines(stream_ref, dot(analy_x_ref[...], (phi * phi * phi).astype(BF16)), p)
        return carry

    lax.fori_loop(0, PLANES, cube_plane, 0)
    phi = dot(synth_x_ref[...], last_ref[...])
    last_phi_ref[...] = phi
    last_back(dot(analy_x_ref[...], (phi * phi * phi).astype(BF16)), points_ref)
    back(phi_send, phi_recv, phi_sems, cube_recv, cube_sems)

    planes_of(vel_send, vel_recv, vel_sems)

    def flux_plane(p, carry):
        flux = dot(synth_x_ref[...], plane_ref[p]) * work_ref[p]
        keep_lines(stream_ref, dot(analy_x_ref[...], flux.astype(BF16)), p)
        return carry

    lax.fori_loop(0, PLANES, flux_plane, 0)
    flux = dot(synth_x_ref[...], last_ref[...]) * last_phi_ref[...]
    last_back(dot(analy_x_ref[...], flux.astype(BF16)), points_ref)
    back(vel_send, vel_recv, vel_sems, flux_recv, flux_sems)

    def squares_at(h, start):
        return wave_squares(place, spans * 2, streams * 16, spans, streams, h, start)

    eig = eig_ref[:, 0:1]

    def times_both(vector):
        return dot(both_table[...], vector[0:rows].astype(BF16)) + ends_ref[2, :, 0:1] * vector[rows:cheb]

    for g in range(2):
        all_chunks(place, phi_send, cube_recv, cube_sems, g).wait_recv()
        if g == 0:
            last_edge(place, cube_recv, analy_z_ref, edge_ref)
        for h in range(HALVES):
            at = lanes_of(g)
            phi = solve_ref[h, :, at]
            cube = dot(analy_y_ref[:, 0:rows], unpack_rows(cube_recv, h, at)) + ends_ref[0, :, 0:1] * edge_ref[h, 0:1, at]
            lap = times_both((eig - squares_at(h, g * WIDE)) * (cube - (1.0 + stabilizer) * phi))
            solve_ref[h, :, at] = (phi / time_step + mobility * lap) / (capillary * mobility)
    for g in range(2):
        all_chunks(place, vel_send, flux_recv, flux_sems, g).wait_recv()
        if g == 0:
            last_edge(place, flux_recv, analy_z_ref, edge_ref)
        for h in range(HALVES):
            at = lanes_of(g)
            shifted = eig - squares_at(h, g * WIDE)
            slope = dot(slope_ref[:, 0:rows], unpack_rows(flux_recv, h, at)) + ends_ref[1, :, 0:1] * edge_ref[h, 0:1, at]
            forcing = solve_ref[h, :, at] - 8.0 / (cheb - 1) / (capillary * mobility) * slope
            middle = times_both(forcing / (shifted - screen_low))
            out_ref[h, :, at] = (middle / (shifted - screen_high)).astype(BF16)
    for g in range(2):
        all_chunks(place, phi_send, cube_recv, cube_sems, g).wait_send()
        all_chunks(place, vel_send, flux_recv, flux_sems, g).wait_send()


def finish_kernel(second_ref, basis_ref, out_ref):
    half, spans, _ = out_ref.shape
    for start in range(0, LANES, BLOCK):
        result = lax.dot_general(
            second_ref[0, :, start : start + BLOCK], basis_ref[...], (((0,), (1,)), ((), ())), preferred_element_type=F32
        )
        for k in range(half):
            off = BASE + k * WINDOW
            low, high = max(off, start), min(off + spans, start + BLOCK)
            if low < high:
                out_ref[k, low - off : high - off, :] = result[low - start : high - start]


def per_device(phi_hat, vel_hat, helm_basis, helm_dual, helm_rates):
    span_count = lax.axis_size("nz")
    stream_count = lax.axis_size("nx")
    span_local, stream_local, cheb = phi_hat.shape
    half = stream_local // HALVES
    s_x, a_x = fourier_tables(stream_local * stream_count, NX)
    s_z, a_z = fourier_tables(span_local * span_count, NZ)
    s_y, a_y, d_y = chebyshev_tables(cheb)

    points = np.pad(s_y.T, ((0, -cheb % 8), (0, 0)))
    slope = (d_y.astype(np.float64).T @ a_y.astype(np.float64).T).astype(np.float32).astype(BF)
    order = np.arange(stream_local * stream_count).reshape(stream_count, HALVES, half).transpose(2, 0, 1).reshape(-1)
    synth_x = np.ascontiguousarray(s_x.T[:, order])
    analy_x = np.ascontiguousarray(a_x.T[order])
    synth_z = np.pad(s_z.reshape(span_count, span_local, NZ), ((0, 0), (0, TILE - span_local), (0, 0))).reshape(-1, NZ)
    analy_z = np.pad(a_z.reshape(NZ, span_count, span_local), ((0, 0), (0, 0), (0, TILE - span_local))).reshape(NZ, -1)

    large = [jnp.transpose(phi_hat, (1, 0, 2)), jnp.transpose(vel_hat, (1, 0, 2))]
    tables = (points, np.ascontiguousarray(synth_z.T), synth_z, synth_x, analy_x, analy_z, np.ascontiguousarray(a_y.T), slope)
    large += [jnp.asarray(table) for table in tables] + [helm_dual, helm_basis]
    modes_x = stream_local * stream_count
    chunk = pltpu.VMEM((DEVICES, 8, LANES), BF16)
    sems = pltpu.SemaphoreType.DMA((2, 2))
    second = pl.pallas_call(
        kernel,
        out_shape=jax.ShapeDtypeStruct((HALVES, cheb, LANES), BF16),
        in_specs=[pl.BlockSpec(memory_space=pl.ANY)] * len(large) + [pl.BlockSpec(memory_space=pltpu.VMEM)],
        out_specs=pl.BlockSpec(memory_space=pltpu.VMEM),
        scratch_shapes=[pltpu.VMEM(large[0].shape, BF16)]
        + [pltpu.VMEM(table.shape, BF16) for table in large[2:]]
        + [
            pltpu.VMEM((LANES, cheb), F32),
            pltpu.VMEM((PLANES, NX, NZ), F32),
            pltpu.VMEM((HALVES, cheb, LANES), F32),
            pltpu.VMEM((PLANES, modes_x, NZ), BF16),
            pltpu.VMEM((2, 6 * 256, TILE), F32),
            pltpu.VMEM((11 * 256, NZ), BF16),
            pltpu.VMEM((NZ // TILE, 11 * 256, TILE), F32),
            pltpu.VMEM((TILE, TILE), F32),
            pltpu.VMEM((modes_x, TILE), BF16),
            pltpu.VMEM((NX, TILE), F32),
            pltpu.VMEM((HALVES, 8, LANES), F32),
            pltpu.VMEM((cheb, TILE), F32),
            pltpu.VMEM((cheb, cheb - 1), BF16),
            pltpu.VMEM((3, cheb, TILE), F32),
        ]
        + [chunk] * 6
        + [
            pltpu.SemaphoreType.DMA((len(large) - 2,)), pltpu.SemaphoreType.DMA, pltpu.SemaphoreType.DMA,
            sems, sems, sems, sems,
        ],
        compiler_params=pltpu.CompilerParams(collective_id=0, has_side_effects=True, vmem_limit_bytes=60 << 20),
    )(*large, helm_rates.reshape(1, cheb))
    result = pl.pallas_call(
        finish_kernel,
        out_shape=jax.ShapeDtypeStruct((stream_local, span_local, cheb), F32),
        grid=(HALVES,),
        in_specs=[pl.BlockSpec((1, cheb, LANES), lambda h: (h, 0, 0)), pl.BlockSpec((cheb, cheb), lambda h: (0, 0))],
        out_specs=pl.BlockSpec((half, span_local, cheb), lambda h: (h, 0, 0)),
        compiler_params=pltpu.CompilerParams(vmem_limit_bytes=40 << 20),
    )(second, helm_basis)
    return jnp.transpose(result, (1, 0, 2))


def solution(mesh):
    placed = (P("nz", "nx", None), P("nz", "nx", None), P(), P(), P())
    return jax.shard_map(
        per_device, mesh=mesh, in_specs=placed, out_specs=P("nz", "nx", None), check_vma=False
    )
```

time: 134 us -> 117 us (0.87)
  Pallas kernels: 131 us -> 114 us
    pallas_call x1, Pallas kernels: 127 us -> 110 us  [per_device(): pl.pallas_call(kernel, out_shape=jax.ShapeDtypeStruct((HALVES, cheb, LANE...]
where the time goes in v3:
time: 117 us
  Pallas kernels  114 us (97%)
  local copies, waits for them, and re-layouts  2.86 us (2%)
    pallas_call x1, Pallas kernels, per_device(): pl.pallas_call(kernel, out_shape=jax.ShapeDtypeStruct((HALVES, cheb, LANE...  110 us
    pallas_call x1, Pallas kernels, per_device(): pl.pallas_call(finish_kernel, out_shape=jax.ShapeDtypeStruct((stream_loca...  4.32 us

profile of v3, /device:TPU:1, one launch (start us, length us, event | category | flops | bytes accessed | tf_op | source)
XLA Modules:
  0.0 116.9 jit_solution(13292963064581468888)
XLA Ops:
  0.0 1.3 %reshape.3.rates_ref = f32[1,513]{1,0:T(1,128)} reshape(f32[513]{0:T(1024)} %param.17) | data formatting | bytes 4104 | tf_op jit(solution)/shard_map/reshape | solution.py:567
  1.3 0.0 copy-start.1
  1.3 109.7 %shard_map.127.second_ref = bf16[2,513,1024]{2,1,0:T(8,128)(2,1)} custom-call(bf16[22,86,513]{2,1,0:T(8,128)(2,1)} %bitcast.3, bf16[22,86,513]{2,1,0:T(8,128)(2,1)} %bitcast.4, bf16[520,513]{1,0:T(8,128)(2,1)} %constant.16.clone.points_hbm, bf16[512,512]{1,0:T(8,128)(2,1)} %constant.17.clone.synth_zt_hbm, bf16[512,512]{1,0:T(8,128)(2,1)} %constant.18.clone.synth_z_hbm, ...), custom_call_target="tpu_custom_call" | custom-call | tf_op jit(solution)/shard_map/pallas_call | solution.py:538
  111.0 0.0 copy-done.1
  111.0 0.0 copy-start
  111.0 1.6 %copy-done = bf16[2,513,1024]{2,1,0:T(8,128)(2,1)S(1)} copy-done((bf16[2,513,1024]{2,1,0:T(8,128)(2,1)S(1)}, bf16[2,513,1024]{2,1,0:T(8,128)(2,1)}, u32[]{:S(2)}) %copy-start) | copy-done | bytes 2101272
  112.6 4.3 %shard_map.128 = f32[22,86,513]{2,1,0:T(8,128)} custom-call(bf16[2,513,1024]{2,1,0:T(8,128)(2,1)S(1)} %copy-done, bf16[513,513]{1,0:T(8,128)(2,1)S(1)} %copy-done.1), custom_call_target="tpu_custom_call" | custom-call | tf_op jit(solution)/shard_map/pallas_call | solution.py:568
Async XLA Ops:
  1.3 109.7 %copy-start.1 = (bf16[513,513]{1,0:T(8,128)(2,1)S(1)}, bf16[513,513]{1,0:T(8,128)(2,1)}, u32[]{:S(2)}) copy-start(bf16[513,513]{1,0:T(8,128)(2,1)} %basis_ref.1) | copy-start | bytes 1579018
  111.0 1.6 %copy-start = (bf16[2,513,1024]{2,1,0:T(8,128)(2,1)S(1)}, bf16[2,513,1024]{2,1,0:T(8,128)(2,1)}, u32[]{:S(2)}) copy-start(bf16[2,513,1024]{2,1,0:T(8,128)(2,1)} %shard_map.127.second_ref) | copy-start | bytes 6303748

commit v4 on v3

--- a/solution.py
+++ b/solution.py
@@ -21,7 +21,7 @@
 
 PLANES = 4
 HALVES = 2
-WINDOW = 88
+WINDOW = 86
 LANES = 1024
 TILE = 128
 BF = ml_dtypes.bfloat16
@@ -77,7 +77,8 @@
 DEVICES = 128
 BLOCK = 256
 WIDE = 512
-BASE = LANES - 11 * WINDOW
+CUTS = (0, 512, 896, 1024)
+BASE = 11
 
 
 class Place:
@@ -118,7 +119,7 @@
 
 
 def lanes_of(g):
-    return slice(g * WIDE, (g + 1) * WIDE)
+    return slice(CUTS[g], CUTS[g + 1])
 
 
 def scatter(place, src, dst, sems, own_sem, g):
@@ -251,8 +252,23 @@
         stream_ref[t, pl.ds(p, lines.shape[0], stride=PLANES), :] = lines[:, tile_of(t)]
 
 
-SPARE = 72
 LAST = slice(LANES - TILE, LANES)
+
+
+def join_last(first_ref, second_ref):
+    first, second = first_ref[:, :, LAST].astype(F32), second_ref[:, :, LAST].astype(F32)
+    moved = pltpu.roll(second.reshape(DEVICES * 8, TILE), TILE // 2, 1).reshape(second.shape)
+    second_ref[:, :, LAST] = jnp.where(rows_of(first.shape, 2) < TILE // 2, first, moved).astype(BF16)
+
+
+def split_last(first_ref, second_ref):
+    both = second_ref[:, :, LAST]
+    first_ref[:, :, LAST] = both
+    moved = pltpu.roll(both.astype(F32).reshape(DEVICES * 8, TILE), TILE // 2, 1).reshape(both.shape)
+    second_ref[:, :, LAST] = moved.astype(BF16)
+
+
+SPARE = 11 * WINDOW - CUTS[2]
 
 
 def last_out(place, work_ref, table_ref, rows_ref):
@@ -324,8 +340,8 @@
                 edge_ref[h, 0:1, tile_of(first + 1)] = moved
 
 
-def wave_squares(place, half_span, half_stream, span_local, stream_local, h, start):
-    lane = start - BASE + rows_of((1, WIDE), 1)
+def wave_squares(place, half_span, half_stream, span_local, stream_local, h, g):
+    lane = CUTS[g] - BASE + rows_of((1, CUTS[g + 1] - CUTS[g]), 1)
     k, j = lane // WINDOW, lane % WINDOW
 
     def squared(mode, count):
@@ -341,7 +357,7 @@
     dual_hbm, basis_hbm, rates_ref, out_ref,
     modes_ref, table_y_ref, synth_zt_ref, synth_z_ref, synth_x_ref, analy_x_ref, analy_z_ref, analy_y_ref, slope_ref,
     dual_ref, basis_ref, stage_ref, work_ref, solve_ref, plane_ref, points_ref, lines_ref, stream_ref, rows_ref, last_ref, last_phi_ref,
-    edge_ref, eig_ref, both_table, ends_ref,
+    cube_edge, flux_edge, eig_ref, both_table, ends_ref,
     phi_send, vel_send, phi_recv, vel_recv, cube_recv, flux_recv,
     table_sems, modes_sem, own_sem, phi_sems, vel_sems, cube_sems, flux_sems,
 ):
@@ -372,7 +388,8 @@
 
     stage_ref[...] = jnp.zeros_like(stage_ref)
     rows_ref[...] = jnp.zeros_like(rows_ref)
-    edge_ref[...] = jnp.zeros_like(edge_ref)
+    cube_edge[...] = jnp.zeros_like(cube_edge)
+    flux_edge[...] = jnp.zeros_like(flux_edge)
     modes_copy.wait()
     stage_modes(modes_ref, stage_ref, 0, 0)
     moves["points"].wait()
@@ -394,7 +411,7 @@
             vel_copy = pltpu.make_async_copy(vel_hbm, modes_ref, modes_sem)
             vel_copy.start()
         for h in range(HALVES):
-            solve_ref[h, :, lanes_of(g)] = dot_nt(dual_ref[...], stage_ref[h * WIDE : (h + 1) * WIDE, :].astype(BF16))
+            solve_ref[h, :, g * WIDE : (g + 1) * WIDE] = dot_nt(dual_ref[...], stage_ref[h * WIDE : (h + 1) * WIDE, :].astype(BF16))
 
     vel_copy.wait()
     for g in range(2):
@@ -403,6 +420,8 @@
         if g == 1:
             last_out(place, work_ref, synth_zt_ref, rows_ref)
         pack_chunks(work_ref, vel_send, g)
+    join_last(phi_send, vel_send)
+    for g in (2, 0, 1):
         scatter(place, vel_send, vel_recv, vel_sems, own_sem, g)
 
     for name in ("analy_y", "slope", "basis"):
@@ -414,32 +433,25 @@
     full = dot(dual_ref[...], basis_ref[...])
     both_table[...] = full[:, 0:rows].astype(BF16)
     ends_ref[2] = jnp.broadcast_to(full[:, rows:cheb], (cheb, TILE))
-    eig_ref[0:rows, :] = -jnp.transpose(jnp.broadcast_to(rates_ref[:, 0:rows], (TILE, rows)))
-    eig_ref[rows:cheb, :] = -jnp.broadcast_to(rates_ref[:, rows:cheb], (1, TILE))
+    eig_ref[0:rows, :] = -jnp.transpose(jnp.broadcast_to(rates_ref[...].reshape(1, cheb)[:, 0:rows], (TILE, rows)))
+    eig_ref[rows:cheb, :] = -jnp.broadcast_to(rates_ref[...].reshape(1, cheb)[:, rows:cheb], (1, TILE))
 
     for name in ("synth_z", "synth_x", "analy_x", "analy_z"):
         moves[name].wait()
-    early, late = range(0, 5), range(5, 11)
-
-    def planes_of(send, recv, sems):
-        all_chunks(place, send, recv, sems, 0).wait_recv()
-        fill_windows(recv, lines_ref, early)
-        synth_z(lines_ref, synth_z_ref, plane_ref, points_ref, early)
-        all_chunks(place, send, recv, sems, 1).wait_recv()
-        fill_windows(recv, lines_ref, late)
-        synth_z(lines_ref, synth_z_ref, plane_ref, points_ref, late)
-        last_in(recv, points_ref, last_ref)
-
-    def back(send, recv, sems, to, to_sems):
-        all_chunks(place, send, recv, sems, 0).wait_send()
-        all_chunks(place, send, recv, sems, 1).wait_send()
-        analyse_z(stream_ref, lines_ref, analy_z_ref, send, range(0, 6))
-        last_fill(points_ref, send)
-        scatter(place, send, to, to_sems, own_sem, 0)
-        analyse_z(stream_ref, lines_ref, analy_z_ref, send, range(6, 11))
-        scatter(place, send, to, to_sems, own_sem, 1)
-
-    planes_of(phi_send, phi_recv, phi_sems)
+    def planes_of(recv, ks):
+        fill_windows(recv, lines_ref, ks)
+        synth_z(lines_ref, synth_z_ref, plane_ref, points_ref, ks)
+
+    def vel_came(g):
+        all_chunks(place, vel_send, vel_recv, vel_sems, g).wait_recv()
+
+    for g, ks in enumerate((range(0, 5), range(5, 10))):
+        all_chunks(place, phi_send, phi_recv, phi_sems, g).wait_recv()
+        planes_of(phi_recv, ks)
+    vel_came(2)
+    split_last(phi_recv, vel_recv)
+    planes_of(phi_recv, range(10, 11))
+    last_in(phi_recv, points_ref, last_ref)
 
     def cube_plane(p, carry):
         phi = dot(synth_x_ref[...], plane_ref[p])
@@ -451,9 +463,19 @@
     phi = dot(synth_x_ref[...], last_ref[...])
     last_phi_ref[...] = phi
     last_back(dot(analy_x_ref[...], (phi * phi * phi).astype(BF16)), points_ref)
-    back(phi_send, phi_recv, phi_sems, cube_recv, cube_sems)
-
-    planes_of(vel_send, vel_recv, vel_sems)
+    for g in range(2):
+        all_chunks(place, phi_send, phi_recv, phi_sems, g).wait_send()
+    analyse_z(stream_ref, lines_ref, analy_z_ref, phi_send, range(0, 6))
+    last_fill(points_ref, phi_send)
+    scatter(place, phi_send, cube_recv, cube_sems, own_sem, 0)
+    analyse_z(stream_ref, lines_ref, analy_z_ref, phi_send, range(6, 11))
+    scatter(place, phi_send, cube_recv, cube_sems, own_sem, 1)
+
+    vel_came(0)
+    planes_of(vel_recv, range(0, 5))
+    vel_came(1)
+    planes_of(vel_recv, range(5, 11))
+    last_in(vel_recv, points_ref, last_ref)
 
     def flux_plane(p, carry):
         flux = dot(synth_x_ref[...], plane_ref[p]) * work_ref[p]
@@ -463,53 +485,90 @@
     lax.fori_loop(0, PLANES, flux_plane, 0)
     flux = dot(synth_x_ref[...], last_ref[...]) * last_phi_ref[...]
     last_back(dot(analy_x_ref[...], flux.astype(BF16)), points_ref)
-    back(vel_send, vel_recv, vel_sems, flux_recv, flux_sems)
-
-    def squares_at(h, start):
-        return wave_squares(place, spans * 2, streams * 16, spans, streams, h, start)
+    for g in range(3):
+        all_chunks(place, vel_send, vel_recv, vel_sems, g).wait_send()
+    analyse_z(stream_ref, lines_ref, analy_z_ref, vel_send, range(0, 6))
+    last_fill(points_ref, vel_send)
+    scatter(place, vel_send, flux_recv, flux_sems, own_sem, 0)
+    analyse_z(stream_ref, lines_ref, analy_z_ref, vel_send, range(6, 11))
+    join_last(phi_send, vel_send)
+    scatter(place, vel_send, flux_recv, flux_sems, own_sem, 2)
+    scatter(place, vel_send, flux_recv, flux_sems, own_sem, 1)
+
+    def squares_at(h, g):
+        return wave_squares(place, spans * 2, streams * 16, spans, streams, h, g)
 
     eig = eig_ref[:, 0:1]
 
     def times_both(vector):
         return dot(both_table[...], vector[0:rows].astype(BF16)) + ends_ref[2, :, 0:1] * vector[rows:cheb]
 
-    for g in range(2):
-        all_chunks(place, phi_send, cube_recv, cube_sems, g).wait_recv()
-        if g == 0:
-            last_edge(place, cube_recv, analy_z_ref, edge_ref)
+    def lap(g):
+        at = lanes_of(g)
         for h in range(HALVES):
-            at = lanes_of(g)
             phi = solve_ref[h, :, at]
-            cube = dot(analy_y_ref[:, 0:rows], unpack_rows(cube_recv, h, at)) + ends_ref[0, :, 0:1] * edge_ref[h, 0:1, at]
-            lap = times_both((eig - squares_at(h, g * WIDE)) * (cube - (1.0 + stabilizer) * phi))
-            solve_ref[h, :, at] = (phi / time_step + mobility * lap) / (capillary * mobility)
-    for g in range(2):
-        all_chunks(place, vel_send, flux_recv, flux_sems, g).wait_recv()
-        if g == 0:
-            last_edge(place, flux_recv, analy_z_ref, edge_ref)
+            cube = dot(analy_y_ref[:, 0:rows], unpack_rows(cube_recv, h, at)) + ends_ref[0, :, 0:1] * cube_edge[h, 0:1, at]
+            part = times_both((eig - squares_at(h, g)) * (cube - (1.0 + stabilizer) * phi))
+            solve_ref[h, :, at] = (phi / time_step + mobility * part) / (capillary * mobility)
+
+    def solve(g):
+        at = lanes_of(g)
         for h in range(HALVES):
-            at = lanes_of(g)
-            shifted = eig - squares_at(h, g * WIDE)
-            slope = dot(slope_ref[:, 0:rows], unpack_rows(flux_recv, h, at)) + ends_ref[1, :, 0:1] * edge_ref[h, 0:1, at]
+            shifted = eig - squares_at(h, g)
+            slope = dot(slope_ref[:, 0:rows], unpack_rows(flux_recv, h, at)) + ends_ref[1, :, 0:1] * flux_edge[h, 0:1, at]
             forcing = solve_ref[h, :, at] - 8.0 / (cheb - 1) / (capillary * mobility) * slope
             middle = times_both(forcing / (shifted - screen_low))
             out_ref[h, :, at] = (middle / (shifted - screen_high)).astype(BF16)
+
+    all_chunks(place, phi_send, cube_recv, cube_sems, 0).wait_recv()
+    last_edge(place, cube_recv, analy_z_ref, cube_edge)
+    lap(0)
+    all_chunks(place, phi_send, cube_recv, cube_sems, 1).wait_recv()
+    lap(1)
+    all_chunks(place, vel_send, flux_recv, flux_sems, 0).wait_recv()
+    last_edge(place, flux_recv, analy_z_ref, flux_edge)
+    solve(0)
+    all_chunks(place, vel_send, flux_recv, flux_sems, 2).wait_recv()
+    split_last(cube_recv, flux_recv)
+    lap(2)
+    solve(2)
+    all_chunks(place, vel_send, flux_recv, flux_sems, 1).wait_recv()
+    solve(1)
     for g in range(2):
         all_chunks(place, phi_send, cube_recv, cube_sems, g).wait_send()
+    for g in range(3):
         all_chunks(place, vel_send, flux_recv, flux_sems, g).wait_send()
 
 
-def finish_kernel(second_ref, basis_ref, out_ref):
-    half, spans, _ = out_ref.shape
-    for start in range(0, LANES, BLOCK):
-        result = lax.dot_general(
-            second_ref[0, :, start : start + BLOCK], basis_ref[...], (((0,), (1,)), ((), ())), preferred_element_type=F32
-        )
-        for k in range(half):
-            off = BASE + k * WINDOW
-            low, high = max(off, start), min(off + spans, start + BLOCK)
-            if low < high:
-                out_ref[k, low - off : high - off, :] = result[low - start : high - start]
+def finish_kernel(second_hbm, basis_hbm, out_hbm, second_ref, basis_ref, out_ref, in_sems, out_sems):
+    half, spans = out_ref.shape[0] // HALVES, out_ref.shape[1]
+    table = pltpu.make_async_copy(basis_hbm, basis_ref, in_sems.at[HALVES])
+    table.start()
+    moves = [pltpu.make_async_copy(second_hbm.at[h], second_ref.at[h], in_sems.at[h]) for h in range(HALVES)]
+    for move in moves:
+        move.start()
+    table.wait()
+    parts = []
+    for h in range(HALVES):
+        moves[h].wait()
+        for g in range(2):
+            start = g * WIDE
+            result = lax.dot_general(
+                second_ref[h, :, start : start + WIDE], basis_ref[...], (((0,), (1,)), ((), ())), preferred_element_type=F32
+            )
+            done = []
+            for k in range(half):
+                off = BASE + k * WINDOW
+                low, high = max(off, start), min(off + spans, start + WIDE)
+                if low < high:
+                    out_ref[h * half + k, low - off : high - off, :] = result[low - start : high - start]
+                    if high == off + spans:
+                        done.append(h * half + k)
+            rows = slice(done[0], done[-1] + 1)
+            parts.append(pltpu.make_async_copy(out_ref.at[rows], out_hbm.at[rows], out_sems.at[h * 2 + g]))
+            parts[-1].start()
+    for part in parts:
+        part.wait()
 
 
 def per_device(phi_hat, vel_hat, helm_basis, helm_dual, helm_rates):
@@ -534,7 +593,7 @@
     large += [jnp.asarray(table) for table in tables] + [helm_dual, helm_basis]
     modes_x = stream_local * stream_count
     chunk = pltpu.VMEM((DEVICES, 8, LANES), BF16)
-    sems = pltpu.SemaphoreType.DMA((2, 2))
+    two, three = pltpu.SemaphoreType.DMA((2, 2)), pltpu.SemaphoreType.DMA((3, 2))
     second = pl.pallas_call(
         kernel,
         out_shape=jax.ShapeDtypeStruct((HALVES, cheb, LANES), BF16),
@@ -554,6 +613,7 @@
             pltpu.VMEM((modes_x, TILE), BF16),
             pltpu.VMEM((NX, TILE), F32),
             pltpu.VMEM((HALVES, 8, LANES), F32),
+            pltpu.VMEM((HALVES, 8, LANES), F32),
             pltpu.VMEM((cheb, TILE), F32),
             pltpu.VMEM((cheb, cheb - 1), BF16),
             pltpu.VMEM((3, cheb, TILE), F32),
@@ -561,17 +621,21 @@
         + [chunk] * 6
         + [
             pltpu.SemaphoreType.DMA((len(large) - 2,)), pltpu.SemaphoreType.DMA, pltpu.SemaphoreType.DMA,
-            sems, sems, sems, sems,
+            two, three, two, three,
         ],
         compiler_params=pltpu.CompilerParams(collective_id=0, has_side_effects=True, vmem_limit_bytes=60 << 20),
-    )(*large, helm_rates.reshape(1, cheb))
+    )(*large, helm_rates)
+    shape = (stream_local, span_local, cheb)
     result = pl.pallas_call(
         finish_kernel,
-        out_shape=jax.ShapeDtypeStruct((stream_local, span_local, cheb), F32),
-        grid=(HALVES,),
-        in_specs=[pl.BlockSpec((1, cheb, LANES), lambda h: (h, 0, 0)), pl.BlockSpec((cheb, cheb), lambda h: (0, 0))],
-        out_specs=pl.BlockSpec((half, span_local, cheb), lambda h: (h, 0, 0)),
-        compiler_params=pltpu.CompilerParams(vmem_limit_bytes=40 << 20),
+        out_shape=jax.ShapeDtypeStruct(shape, F32),
+        in_specs=[pl.BlockSpec(memory_space=pl.ANY)] * 2,
+        out_specs=pl.BlockSpec(memory_space=pl.ANY),
+        scratch_shapes=[
+            pltpu.VMEM((HALVES, cheb, LANES), BF16), pltpu.VMEM((cheb, cheb), BF16), pltpu.VMEM(shape, F32),
+            pltpu.SemaphoreType.DMA((HALVES + 1,)), pltpu.SemaphoreType.DMA((HALVES * 2,)),
+        ],
+        compiler_params=pltpu.CompilerParams(vmem_limit_bytes=60 << 20),
     )(second, helm_basis)
     return jnp.transpose(result, (1, 0, 2))
 

time: 117 us -> 110 us (0.940)
  Pallas kernels: 114 us -> 109 us
  local copies, waits for them, and re-layouts: 2.86 us -> 0 us
    pallas_call x1, Pallas kernels: 110 us -> 104 us  [per_device(): pl.pallas_call(kernel, out_shape=jax.ShapeDtypeStruct((HALVES, cheb, LANE...]
    unnamed x4 -> x0, local copies, waits for them, and re-layouts: 1.6 us -> none
    reshape x1 -> x0, local copies, waits for them, and re-layouts: 1.27 us -> none  [per_device(): helm_rates.reshape(1, cheb)]
where the time goes in v4:
time: 110 us
  Pallas kernels  109 us (99%)
    pallas_call x1, Pallas kernels, per_device(): pl.pallas_call(kernel, out_shape=jax.ShapeDtypeStruct((HALVES, cheb, LANE...  104 us
    pallas_call x1, Pallas kernels, per_device(): pl.pallas_call(finish_kernel, out_shape=jax.ShapeDtypeStruct(shape, F32),...  5.28 us

profile of v4, /device:TPU:1, one launch (start us, length us, event | category | flops | bytes accessed | tf_op | source)
XLA Modules:
  0.0 109.5 jit_solution(7000912181734795623)
XLA Ops:
  0.0 104.1 %shard_map.127.second_hbm = bf16[2,513,1024]{2,1,0:T(8,128)(2,1)} custom-call(bf16[22,86,513]{2,1,0:T(8,128)(2,1)} %bitcast.3, bf16[22,86,513]{2,1,0:T(8,128)(2,1)} %bitcast.4, bf16[520,513]{1,0:T(8,128)(2,1)} %constant.16.clone.points_hbm, bf16[512,512]{1,0:T(8,128)(2,1)} %constant.17.clone.synth_zt_hbm, bf16[512,512]{1,0:T(8,128)(2,1)} %constant.18.clone.synth_z_hbm, ...), custom_call_target="tpu_custom_call" | custom-call | tf_op jit(solution)/shard_map/pallas_call | solution.py:597
  104.1 5.3 %shard_map.128 = f32[22,86,513]{2,1,0:T(8,128)} custom-call(bf16[2,513,1024]{2,1,0:T(8,128)(2,1)} %shard_map.127.second_hbm, bf16[513,513]{1,0:T(8,128)(2,1)} %basis_hbm.3), custom_call_target="tpu_custom_call" | custom-call | tf_op jit(solution)/shard_map/pallas_call | solution.py:629

commit v5 on v4

--- a/solution.py
+++ b/solution.py
@@ -602,7 +602,7 @@
         scratch_shapes=[pltpu.VMEM(large[0].shape, BF16)]
         + [pltpu.VMEM(table.shape, BF16) for table in large[2:]]
         + [
-            pltpu.VMEM((LANES, cheb), F32),
+            pltpu.VMEM((LANES + 16, cheb), F32),
             pltpu.VMEM((PLANES, NX, NZ), F32),
             pltpu.VMEM((HALVES, cheb, LANES), F32),
             pltpu.VMEM((PLANES, modes_x, NZ), BF16),

time: 110 us -> 110 us (level)
  no operation moved by 1% of the time
where the time goes in v5:
time: 110 us
  Pallas kernels  109 us (99%)
    pallas_call x1, Pallas kernels, per_device(): pl.pallas_call(kernel, out_shape=jax.ShapeDtypeStruct((HALVES, cheb, LANE...  104 us
    pallas_call x1, Pallas kernels, per_device(): pl.pallas_call(finish_kernel, out_shape=jax.ShapeDtypeStruct(shape, F32),...  5.28 us

profile of v5, /device:TPU:1, one launch (start us, length us, event | category | flops | bytes accessed | tf_op | source)
XLA Modules:
  0.0 109.5 jit_solution(10420327124682745521)
XLA Ops:
  0.0 104.1 %shard_map.127.second_hbm = bf16[2,513,1024]{2,1,0:T(8,128)(2,1)} custom-call(bf16[22,86,513]{2,1,0:T(8,128)(2,1)} %bitcast.3, bf16[22,86,513]{2,1,0:T(8,128)(2,1)} %bitcast.4, bf16[520,513]{1,0:T(8,128)(2,1)} %constant.16.clone.points_hbm, bf16[512,512]{1,0:T(8,128)(2,1)} %constant.17.clone.synth_zt_hbm, bf16[512,512]{1,0:T(8,128)(2,1)} %constant.18.clone.synth_z_hbm, ...), custom_call_target="tpu_custom_call" | custom-call | tf_op jit(solution)/shard_map/pallas_call | solution.py:597
  104.1 5.3 %shard_map.128 = f32[22,86,513]{2,1,0:T(8,128)} custom-call(bf16[2,513,1024]{2,1,0:T(8,128)(2,1)} %shard_map.127.second_hbm, bf16[513,513]{1,0:T(8,128)(2,1)} %basis_hbm.3), custom_call_target="tpu_custom_call" | custom-call | tf_op jit(solution)/shard_map/pallas_call | solution.py:629
